TPU v7x, 128 devices: a whole 4x4x4 slice. The times are simulated.
128 devices in a mesh: win: 2 (over x_hi), seq: 16 (over y, x_lo, core), head: 4 (over z).
Axes of the slice: x: 4 (x_hi: 2, x_lo: 2; x = x_hi * 2 + x_lo), y: 4, z: 4, core: 2. Of those that a mesh axis runs over, the one named last changes fastest.
Arguments:
- queries: bfloat16 [8192, 3072], P(('win', 'seq'), 'head'), parts along dimension 0, may hold values from -28 to 28
- keys_in: bfloat16 [8192, 3072], P(('win', 'seq'), 'head'), parts along dimension 0, may hold values from -28 to 28
- values_in: bfloat16 [8192, 3072], P(('win', 'seq'), 'head'), parts along dimension 0, may hold values from -6 to 6
- forward_out: bfloat16 [8192, 3072], P(('win', 'seq'), 'head'), parts along dimension 0, may hold values from -6 to 6
- grad_out: bfloat16 [8192, 3072], P(('win', 'seq'), 'head'), parts along dimension 0, may hold values from -6 to 6
- lengths: int32 [16], P('win'), parts along dimension 0, may hold values from 1 to 2048, 4096 in all
- query_block: int32 [64], P(('win', 'seq')), parts along dimension 0, may hold values from 0 to 31, each once
Outputs:
- grad_query: bfloat16 [8192, 3072], P(('win', 'seq'), 'head'), parts along dimension 0
- grad_key: bfloat16 [8192, 3072], P(('win', 'seq'), 'head'), parts along dimension 0
- grad_value: bfloat16 [8192, 3072], P(('win', 'seq'), 'head'), parts along dimension 0
There are 2 independent parts, one for each index of `win`. A program takes and returns all parts, laid end to end along the dimension named above; each array names one. Nothing has to cross between parts.
Inputs may be any that keep to these rules, and one draw needn't show every extreme that they name: `lengths`: whole numbers that sum to 4096; the largest is exactly 2048. `query_block`: each number once.
All inputs are finite; a program needn't handle non-finite values.
Results may differ from a plain program's by a relative error of at most 0.0051.
Values may be sent and summed in bfloat16 or wider, within the bound.
No kernel may reach another device: no remote copies, remote signals or barrier semaphores. Data moves between devices by JAX's collectives and lax.ppermute only.
A program may use at most 128 MiB of HBM per device.

v0:
```python
import math

import jax
import jax.numpy as jnp
from jax import lax
from jax.experimental import pallas as pl
from jax.experimental.pallas import tpu as pltpu
from jax.sharding import PartitionSpec as P

HD = 128
QBLK = 128
CHUNK = 256
TILE = 2 * QBLK
GROUP = 3
SCALE = HD ** (-0.5)
RATE = SCALE * math.log2(math.e)
FLOOR = -1e30
EXTRA = 16

smem = pl.BlockSpec(memory_space=pltpu.SMEM)
vmem = pl.BlockSpec(memory_space=pltpu.VMEM)
params = pltpu.CompilerParams(vmem_limit_bytes=40 * 1024 * 1024)


def dot(a, b):
    return jnp.dot(a, b, preferred_element_type=jnp.float32)


def pack_kernel(ids_ref, k_ref, v_ref, q_ref, out_ref):
    rows = k_ref.shape[0]
    heads = k_ref.shape[1] // HD
    for slot in range(out_ref.shape[0]):
        for i, ref in enumerate((k_ref, v_ref, q_ref)):
            at = slice(i * rows, (i + 1) * rows)
            if slot < heads:
                out_ref[slot, at, :] = ref[:, slot * HD : (slot + 1) * HD]
            else:
                out_ref[slot, at, :] = jnp.zeros((rows, HD), out_ref.dtype)
        out_ref[slot, 3 * rows :, :] = ids_ref[...]


def pack(ids, k, v, q, chips):
    rows = k.shape[0]
    return pl.pallas_call(
        pack_kernel,
        out_shape=jax.ShapeDtypeStruct((chips, 3 * rows + EXTRA, HD), k.dtype),
        in_specs=[vmem] * 4,
        out_specs=vmem,
        name="pack",
    )(ids, k, v, q)


def prepare_kernel(
    core_ref, order_ref, count_ref, list_ref, first_ref, other_ref, key_code, query_code,
    keys, keys_t, values, qs, qt, level_ref, raw,
):
    core = core_ref[0]
    chips = first_ref.shape[0]
    tiles = query_code.shape[0]

    def place(i, carry):
        mine, theirs = 2 * i + core, 2 * i + 1 - core
        for spot, ref in ((mine, first_ref), (theirs, other_ref)):
            k = ref[i, :CHUNK, :]
            keys[spot, :, :HD] = k
            keys[spot, :, HD:] = key_code[spot]
            keys_t[spot] = k.T
            values[spot, :, :HD] = ref[i, CHUNK : 2 * CHUNK, :]
            values[spot, :, HD:] = jnp.full((CHUNK, HD), -1, jnp.bfloat16)
        return carry

    lax.fori_loop(0, chips, place, 0)
    keys[2 * chips] = jnp.ones((CHUNK, 2 * HD), jnp.bfloat16)

    def tile(t, carry):
        for slot in range(2):
            block = order_ref[2 * t + slot]
            at = pl.multiple_of(2 * CHUNK + block % 2 * QBLK, QBLK)
            q = first_ref[block // 2, pl.ds(at, QBLK), :]
            rows = slice(slot * QBLK, (slot + 1) * QBLK)
            qs[t, rows, :] = q
            qt[t, :HD, rows] = q.T
        qt[t, HD:, :] = query_code[t].T
        steps = (count_ref[t] + GROUP - 1) // GROUP

        def score(i):
            i = jnp.minimum(i, steps - 1)
            for u in range(GROUP):
                raw[i % 2, u] = dot(keys[list_ref[t, GROUP * i + u]], qt[t])

        score(0)

        def totals(i, carry):
            top, total = carry
            s = raw[i % 2].reshape(GROUP * 4, 8, 8, TILE)
            new_top = jnp.maximum(top, jnp.max(jnp.max(s, axis=1), axis=0))
            added = jnp.sum(jnp.sum(jnp.exp2((s - new_top) * RATE), axis=1), axis=0)
            score(i + 1)
            return new_top, total * jnp.exp2((top - new_top) * RATE) + added

        top, total = lax.fori_loop(
            0, steps, totals,
            (jnp.full((8, TILE), FLOOR, jnp.float32), jnp.zeros((8, TILE), jnp.float32)),
        )
        row_top = jnp.max(top, axis=0, keepdims=True)
        row_sum = jnp.sum(total * jnp.exp2((top - row_top) * RATE), axis=0, keepdims=True)
        level_ref[t] = row_top + jnp.log2(row_sum) * (1.0 / RATE)
        return carry

    lax.fori_loop(0, tiles, tile, 0)


def prepare(core, order, count, chunk_list, first, other, key_code, query_code):
    chips = first.shape[0]
    blocks, tiles = 2 * chips, chips
    pairs = blocks * QBLK * 2048
    bf16 = jnp.bfloat16
    return pl.pallas_call(
        prepare_kernel,
        out_shape=(
            jax.ShapeDtypeStruct((blocks + 1, CHUNK, 2 * HD), bf16),
            jax.ShapeDtypeStruct((blocks, HD, CHUNK), bf16),
            jax.ShapeDtypeStruct((blocks, CHUNK, 2 * HD), bf16),
            jax.ShapeDtypeStruct((tiles, TILE, HD), bf16),
            jax.ShapeDtypeStruct((tiles, 2 * HD, TILE), bf16),
            jax.ShapeDtypeStruct((tiles, 1, TILE), jnp.float32),
        ),
        in_specs=[smem] * 4 + [vmem] * 4,
        out_specs=(vmem,) * 6,
        scratch_shapes=[pltpu.VMEM((2, GROUP, CHUNK, TILE), jnp.float32)],
        compiler_params=params,
        cost_estimate=pl.CostEstimate(
            flops=4 * pairs * HD, bytes_accessed=8 * 2**20, transcendentals=pairs
        ),
        name="prepare",
    )(core, order, count, chunk_list, first, other, key_code, query_code)


def grads_kernel(
    core_ref, order_ref, count_ref, list_ref,
    second_ref, keys, keys_t, values, qs, qt, level_ref,
    dq_ref, keep_ref, send_ref,
    gs, gt, acc_k, acc_v, acc_q,
):
    core = core_ref[0]
    chips = second_ref.shape[0]
    tiles = qs.shape[0]

    def clear(i, carry):
        acc_k[i] = jnp.zeros((CHUNK, HD), jnp.float32)
        acc_v[i] = jnp.zeros((CHUNK, HD), jnp.float32)
        return carry

    lax.fori_loop(0, 2 * chips, clear, 0)
    gt[HD + EXTRA :, :] = jnp.zeros((HD - EXTRA, TILE), jnp.bfloat16)

    def tile(t, carry):
        a, b = order_ref[2 * t], order_ref[2 * t + 1]
        count = count_ref[t]
        for slot, block in ((0, a), (1, b)):
            at = pl.multiple_of(block % 2 * QBLK, QBLK)
            g = second_ref[block // 2, pl.ds(at, QBLK), :]
            rows = slice(slot * QBLK, (slot + 1) * QBLK)
            gs[rows, :] = g
            gt[:HD, rows] = g.T
            at = pl.multiple_of(CHUNK + block % 2 * EXTRA, EXTRA)
            gt[HD : HD + EXTRA, rows] = second_ref[block // 2, pl.ds(at, EXTRA), :]
        acc_q[...] = jnp.zeros_like(acc_q)
        level = level_ref[t]

        def some(first, number):
            spots = [list_ref[t, first + u] for u in range(number)]
            scores = [dot(keys[spot], qt[t]) for spot in spots]
            slopes = [dot(values[spot], gt[...]) for spot in spots]
            low = []
            for u, spot in enumerate(spots):
                p = jnp.exp2((scores[u] - level) * RATE)
                s = (p * slopes[u]).astype(jnp.bfloat16)
                acc_v[spot] += dot(p.astype(jnp.bfloat16), gs[...])
                acc_k[spot] += dot(s, qs[t])
                low.append(s)
            left = jnp.concatenate([keys_t[spot] for spot in spots], axis=1)
            acc_q[...] += dot(left, jnp.concatenate(low, axis=0))

        def step(i, carry):
            some(GROUP * i, GROUP)
            return carry

        full = count // GROUP
        lax.fori_loop(0, full, step, 0)
        for rest in range(1, GROUP):
            pl.when(count - GROUP * full == rest)(lambda: some(GROUP * full, rest))

        result = (acc_q[...] * SCALE).T.astype(jnp.bfloat16)
        for slot, block in ((0, a), (1, b)):
            at = pl.multiple_of(block % 2 * QBLK, QBLK)
            dq_ref[block // 2, pl.ds(at, QBLK), :] = result[slot * QBLK : (slot + 1) * QBLK]
        return carry

    lax.fori_loop(0, tiles, tile, 0)

    def hand_out(i, carry):
        mine, theirs = 2 * i + core, 2 * i + 1 - core
        keep_ref[i, :CHUNK] = acc_k[mine] * SCALE
        keep_ref[i, CHUNK:] = acc_v[mine]
        send_ref[i, :CHUNK] = (acc_k[theirs] * SCALE).astype(jnp.bfloat16)
        send_ref[i, CHUNK:] = acc_v[theirs].astype(jnp.bfloat16)
        return carry

    lax.fori_loop(0, chips, hand_out, 0)


def grads(core, order, count, chunk_list, second, keys, keys_t, values, qs, qt, level):
    chips = second.shape[0]
    blocks = 2 * chips
    pairs = blocks * QBLK * 2048
    return pl.pallas_call(
        grads_kernel,
        out_shape=(
            jax.ShapeDtypeStruct((chips, TILE, HD), jnp.bfloat16),
            jax.ShapeDtypeStruct((chips, 2 * CHUNK, HD), jnp.float32),
            jax.ShapeDtypeStruct((chips, 2 * CHUNK, HD), jnp.bfloat16),
        ),
        in_specs=[smem] * 4 + [vmem] * 7,
        out_specs=(vmem,) * 3,
        scratch_shapes=[
            pltpu.VMEM((TILE, HD), jnp.bfloat16),
            pltpu.VMEM((2 * HD, TILE), jnp.bfloat16),
            pltpu.VMEM((blocks, CHUNK, HD), jnp.float32),
            pltpu.VMEM((blocks, CHUNK, HD), jnp.float32),
            pltpu.VMEM((HD, TILE), jnp.float32),
        ],
        compiler_params=params,
        cost_estimate=pl.CostEstimate(
            flops=10 * pairs * HD, bytes_accessed=10 * 2**20, transcendentals=pairs
        ),
        name="grads",
    )(core, order, count, chunk_list, second, keys, keys_t, values, qs, qt, level)


def plan(ids, lengths):
    blocks = ids.shape[0]
    ends = jnp.cumsum(lengths)
    offsets = ends - lengths
    starts, stops = (jnp.pad(x, (0, HD - x.shape[0])) for x in (offsets, ends))
    place = jnp.arange(blocks, dtype=jnp.int32)
    lanes = jnp.arange(HD, dtype=jnp.int32)
    key_tokens = jnp.arange(blocks * CHUNK, dtype=jnp.int32)[:, None]
    outside = ((key_tokens < starts) | (key_tokens >= stops)) & (lanes < lengths.shape[0])
    key_code = outside.astype(jnp.bfloat16).reshape(blocks, CHUNK, HD)

    rank = jnp.sum((ids[None, :] < ids[:, None]).astype(jnp.int32), axis=1)
    hit = (rank[None, :] == place[:, None]).astype(jnp.int32)
    order = jnp.sum(hit * place[None, :], axis=1)
    sorted_ids = jnp.sum(hit * ids[None, :], axis=1)
    tokens = (sorted_ids[:, None] * QBLK + jnp.arange(QBLK, dtype=jnp.int32)[None, :])[..., None]
    within = (tokens >= starts) & (tokens < stops)
    query_code = jnp.where(within, FLOOR, 0.0).astype(jnp.bfloat16).reshape(-1, TILE, HD)

    def bounds(token):
        inside = (token[:, None] >= offsets) & (token[:, None] < ends)
        return [jnp.sum(jnp.where(inside, x, 0), axis=1) for x in (offsets, ends)]

    first = bounds(sorted_ids * QBLK)[0] // CHUNK
    last = (bounds(sorted_ids * QBLK + QBLK - 1)[1] - 1) // CHUNK
    needed = (place[None, :] >= first[:, None]) & (place[None, :] <= last[:, None])
    needed = (needed[0::2] | needed[1::2]).astype(jnp.int32)
    count = jnp.sum(needed, axis=1)
    before = jnp.sum(needed[:, None, :] * (place[None, :] < place[:, None]), axis=2)
    slots = jnp.arange(blocks + GROUP, dtype=jnp.int32)
    chosen = (before[:, None, :] == slots[None, :, None]) & (needed[:, None, :] > 0)
    chunk_list = jnp.sum(jnp.where(chosen, place[None, None, :], 0), axis=2)
    chunk_list = jnp.where(slots[None, :] < count[:, None], chunk_list, blocks)
    return order, count, chunk_list, key_code, query_code


def split_in_three(x):
    parts = []
    for _ in range(3):
        part = lax.reduce_precision(x, exponent_bits=8, mantissa_bits=7)
        parts.append(part.astype(jnp.bfloat16))
        x = x - part
    return jnp.stack(parts, axis=-2)


def on_device(queries, keys_in, values_in, forward_out, grad_out, lengths, query_block):
    size = lax.axis_size("seq")
    chips = size // 2
    core = lax.axis_index("seq") % 2
    rows = queries.shape[0]
    heads = queries.shape[1] // HD
    groups = [[2 * i + c for i in range(chips)] for c in range(2)]
    swap = [(i, i ^ 1) for i in range(size)]

    def exchange(x):
        return lax.all_to_all(x, "seq", 0, 0, axis_index_groups=groups)

    ids = jnp.broadcast_to(query_block.astype(jnp.bfloat16)[:, None], (2, HD))
    ids = jnp.pad(ids, ((0, EXTRA - 2), (0, 0)))
    first = exchange(pack(ids, keys_in, values_in, queries, chips))

    delta = jnp.sum(
        (grad_out.astype(jnp.float32) * forward_out.astype(jnp.float32)).reshape(rows, heads, HD),
        axis=2,
    )
    parts = split_in_three(delta.T.reshape(heads, rows // QBLK, QBLK))
    parts = jnp.pad(parts, ((0, 0), (0, 0), (0, EXTRA - 3), (0, 0))).reshape(heads, -1, HD)
    second = jnp.concatenate(
        [grad_out.reshape(rows, heads, HD).transpose(1, 0, 2), parts], axis=1
    )
    second = jnp.pad(second, ((0, chips - heads), (0, 0), (0, 0)))
    first, second = lax.optimization_barrier((first, second))
    second = exchange(second)

    ids = first[:, 3 * rows : 3 * rows + 2, 0].astype(jnp.int32).reshape(-1)
    order, count, chunk_list, key_code, query_code = plan(ids, lengths)
    other = lax.ppermute(first[:, : 2 * rows], "seq", swap)
    core_arg = jnp.full((1,), core, jnp.int32)
    ready = prepare(core_arg, order, count, chunk_list, first, other, key_code, query_code)
    dq, keep, send = grads(core_arg, order, count, chunk_list, second, *ready)

    received = lax.ppermute(send, "seq", swap)
    dq = exchange(dq)
    dkv = exchange((keep + received.astype(jnp.float32)).astype(jnp.bfloat16))

    def by_row(x):
        return x[:heads].transpose(1, 0, 2).reshape(rows, heads * HD)

    return by_row(dq), by_row(dkv[:, :rows]), by_row(dkv[:, rows:])


def solution(mesh):
    spec = P(("win", "seq"), "head")
    in_specs = (spec,) * 5 + (P("win"), P(("win", "seq")))
    return jax.shard_map(
        on_device, mesh=mesh, in_specs=in_specs, out_specs=(spec,) * 3, check_vma=False
    )
```

profile of v0, /device:TPU:4, one launch (start us, length us, event | category | flops | bytes accessed | tf_op | source)
XLA Modules:
  0.0 118.6 jit_solution(3474872629585757885)
XLA Ops:
  0.6 0.7 convert_element_type.87
  1.3 0.7 pad.22.ids_ref
  2.0 2.7 %pack.1 = bf16[8,784,128]{2,1,0:T(8,128)(2,1)} custom-call(bf16[16,128]{1,0:T(8,128)(2,1)} %pad.22.ids_ref, bf16[256,768]{1,0:T(8,128)(2,1)} %k_ref.1, bf16[256,768]{1,0:T(8,128)(2,1)} %v_ref.1, bf16[256,768]{1,0:T(8,128)(2,1)} %q_ref.1), custom_call_target="tpu_custom_call" | custom-call | tf_op jit(solution)/shard_map/pack/pallas_call | solution.py:44
  4.7 5.2 %all-to-all-start = ((bf16[8,784,128]{2,1,0:T(8,128)(2,1)}), bf16[8,784,128]{2,1,0:T(8,128)(2,1)S(1)}, u32[]{:S(2)}, u32[]{:S(2)}) async-start(bf16[8,784,128]{2,1,0:T(8,128)(2,1)} %pack.1), calls=%async_computation | async-start | bytes 3211264 | tf_op jit(solution)/shard_map/all_to_all | solution.py:296
  10.5 0.9 copy.25
  11.4 1.1 convert_multiply_fusion
  12.7 0.9 fusion.2
  13.6 0.7 and_convert_fusion.key_code
  14.3 17.3 %all-to-all-done.first_ref = bf16[8,784,128]{2,1,0:T(8,128)(2,1)S(1)} async-done(((bf16[8,784,128]{2,1,0:T(8,128)(2,1)}), bf16[8,784,128]{2,1,0:T(8,128)(2,1)S(1)}, u32[]{:S(2)}, u32[]{:S(2)}) %all-to-all-start) | async-done | bytes 1605664 | tf_op jit(solution)/shard_map/all_to_all | solution.py:296
  32.5 1.1 slice.28
  33.7 3.5 %all-to-all-start.1 = ((bf16[8,288,128]{2,1,0:T(8,128)(2,1)}), bf16[8,288,128]{2,1,0:T(8,128)(2,1)S(1)}, u32[]{:S(2)}, u32[]{:S(2)}) async-start(bf16[8,288,128]{2,1,0:T(8,128)(2,1)} %fusion.2), calls=%async_computation.1 | async-start | bytes 1179648 | tf_op jit(solution)/shard_map/all_to_all | solution.py:296
  38.3 1.9 %collective-permute-done.other_ref = bf16[8,512,128]{2,1,0:T(8,128)(2,1)S(1)} collective-permute-done((bf16[8,512,128]{2,1,0:T(8,128)(2,1)}, bf16[8,512,128]{2,1,0:T(8,128)(2,1)S(1)}, u32[]{:S(2)}, u32[]{:S(2)}) %collective-permute-start) | collective-permute-done | bytes 1048608 | tf_op jit(solution)/shard_map/ppermute | solution.py:317
  40.2 12.4 %prepare.1 = (bf16[17,256,256]{2,1,0:T(8,128)(2,1)S(1)}, bf16[16,128,256]{2,1,0:T(8,128)(2,1)S(1)}, bf16[16,256,256]{2,1,0:T(8,128)(2,1)S(1)}, bf16[8,256,128]{2...) custom-call(s32[1]{0:T(128)} %bitcast.core_ref, s32[16]{0:T(128)S(1)} %get-tuple-element.34.order_ref, ...), custom_call_target="tpu_custom_call" | custom-call | flops 2147483648 | bytes 8388608 | tf_op jit(solution)/shard_map/prepare/pallas_call | solution.py:118
  52.6 1.4 %copy-done = bf16[17,256,256]{2,1,0:T(8,128)(2,1)} copy-done((bf16[17,256,256]{2,1,0:T(8,128)(2,1)}, bf16[17,256,256]{2,1,0:T(8,128)(2,1)S(1)}, u32[]{:S(2)}) %copy-start) | copy-done | bytes 2228248
  54.0 1.3 %copy-done.2 = bf16[16,256,256]{2,1,0:T(8,128)(2,1)} copy-done((bf16[16,256,256]{2,1,0:T(8,128)(2,1)}, bf16[16,256,256]{2,1,0:T(8,128)(2,1)S(1)}, u32[]{:S(2)}) %copy-start.2) | copy-done | bytes 2097176
  55.3 1.0 copy-done.4
  56.3 1.0 copy-done.6
  57.3 0.8 copy-done.8
  58.1 1.6 %copy-done.1 = bf16[17,256,256]{2,1,0:T(8,128)(2,1)S(1)} copy-done((bf16[17,256,256]{2,1,0:T(8,128)(2,1)S(1)}, bf16[17,256,256]{2,1,0:T(8,128)(2,1)}, u32[]{:S(2)}) %copy-start.1) | copy-done | bytes 2228248
  59.7 1.6 %copy-done.3 = bf16[16,256,256]{2,1,0:T(8,128)(2,1)S(1)} copy-done((bf16[16,256,256]{2,1,0:T(8,128)(2,1)S(1)}, bf16[16,256,256]{2,1,0:T(8,128)(2,1)}, u32[]{:S(2)}) %copy-start.3) | copy-done | bytes 2097176
  61.3 1.2 %copy-done.5 = bf16[16,128,256]{2,1,0:T(8,128)(2,1)S(1)} copy-done((bf16[16,128,256]{2,1,0:T(8,128)(2,1)S(1)}, bf16[16,128,256]{2,1,0:T(8,128)(2,1)}, u32[]{:S(2)}) %copy-start.5) | copy-done | bytes 1048600
  62.6 1.2 %copy-done.7 = bf16[8,256,256]{2,1,0:T(8,128)(2,1)S(1)} copy-done((bf16[8,256,256]{2,1,0:T(8,128)(2,1)S(1)}, bf16[8,256,256]{2,1,0:T(8,128)(2,1)}, u32[]{:S(2)}) %copy-start.7) | copy-done | bytes 1048600
  63.8 1.0 copy-done.9
  64.8 16.8 %grads.1 = (bf16[8,256,128]{2,1,0:T(8,128)(2,1)}, f32[8,512,128]{2,1,0:T(8,128)S(1)}, bf16[8,512,128]{2,1,0:T(8,128)(2,1)}) custom-call(s32[1]{0:T(128)} %bitcast.core_ref, s32[16]{0:T(128)S(1)} %get-tuple-element.34.order_ref, s32[8]{0:T(128)S(1)} %fusion.14.count_ref, s32[8,19]{1,0:T(8,128)S(1)} %fusion.13.list_ref, ...), custom_call_target="tpu_custom_call" | custom-call | flops 5368709120 | bytes 10485760 | tf_op jit(solution)/shard_map/grads/pallas_call | solution.py:217
  81.9 5.5 %all-to-all-start.2 = ((bf16[8,256,128]{2,1,0:T(8,128)(2,1)}), bf16[8,256,128]{2,1,0:T(8,128)(2,1)S(1)}, u32[]{:S(2)}, u32[]{:S(2)}) async-start(bf16[8,256,128]{2,1,0:T(8,128)(2,1)} %get-tuple-element.22), calls=%async_computation.2 | async-start | bytes 1048576 | tf_op jit(solution)/shard_map/all_to_all | solution.py:296
  87.4 2.4 %add_convert_fusion = bf16[8,512,128]{2,1,0:T(8,128)(2,1)} fusion(f32[8,512,128]{2,1,0:T(8,128)S(1)} %get-tuple-element.23, bf16[8,512,128]{2,1,0:T(8,128)(2,1)} %collective-permute-done.1), kind=kLoop, calls=%fused_computation | loop fusion | flops 1572864 | bytes 4194304 | tf_op jit(solution)/shard_map/convert_element_type | solution.py:324
  89.9 8.1 %all-to-all-done.2 = bf16[8,256,128]{2,1,0:T(8,128)(2,1)S(1)} async-done(((bf16[8,256,128]{2,1,0:T(8,128)(2,1)}), bf16[8,256,128]{2,1,0:T(8,128)(2,1)S(1)}, u32[]{:S(2)}, u32[]{:S(2)}) %all-to-all-start.2) | async-done | bytes 524320 | tf_op jit(solution)/shard_map/all_to_all | solution.py:296
  97.9 3.6 %all-to-all-start.3 = ((bf16[8,512,128]{2,1,0:T(8,128)(2,1)}), bf16[8,512,128]{2,1,0:T(8,128)(2,1)S(1)}, u32[]{:S(2)}, u32[]{:S(2)}) async-start(bf16[8,512,128]{2,1,0:T(8,128)(2,1)} %add_convert_fusion), calls=%async_computation.3 | async-start | bytes 2097152 | tf_op jit(solution)/shard_map/all_to_all | solution.py:296
  101.7 0.9 copy.30
  102.6 13.8 %all-to-all-done.3 = bf16[8,512,128]{2,1,0:T(8,128)(2,1)S(1)} async-done(((bf16[8,512,128]{2,1,0:T(8,128)(2,1)}), bf16[8,512,128]{2,1,0:T(8,128)(2,1)S(1)}, u32[]{:S(2)}, u32[]{:S(2)}) %all-to-all-start.3) | async-done | bytes 1048608 | tf_op jit(solution)/shard_map/all_to_all | solution.py:296
  116.6 0.9 copy.32
  117.7 0.9 copy.31
  (59 shorter events, 3.6 us)
Async XLA Ops:
  4.6 5.3 %copy-start.12 = (s32[8]{0:T(128)S(1)}, s32[8]{0:T(128)}, u32[]{:S(2)}) copy-start(s32[8]{0:T(128)} %param.12) | copy-start | bytes 100
  4.6 5.5 %copy-start.10 = (bf16[256,768]{1,0:T(8,128)(2,1)S(1)}, bf16[256,768]{1,0:T(8,128)(2,1)}, u32[]{:S(2)}) copy-start(bf16[256,768]{1,0:T(8,128)(2,1)} %param.11) | copy-start | bytes 1179652
  4.6 5.9 %copy-start.11 = (bf16[256,768]{1,0:T(8,128)(2,1)S(1)}, bf16[256,768]{1,0:T(8,128)(2,1)}, u32[]{:S(2)}) copy-start(bf16[256,768]{1,0:T(8,128)(2,1)} %param.10) | copy-start | bytes 1179652
  4.7 27.0 %all-to-all-start = ((bf16[8,784,128]{2,1,0:T(8,128)(2,1)}), bf16[8,784,128]{2,1,0:T(8,128)(2,1)S(1)}, u32[]{:S(2)}, u32[]{:S(2)}) async-start(bf16[8,784,128]{2,1,0:T(8,128)(2,1)} %pack.1), calls=%async_computation | async-start | bytes 3211264 | tf_op jit(solution)/shard_map/all_to_all | solution.py:296
  33.7 24.4 %all-to-all-start.1 = ((bf16[8,288,128]{2,1,0:T(8,128)(2,1)}), bf16[8,288,128]{2,1,0:T(8,128)(2,1)S(1)}, u32[]{:S(2)}, u32[]{:S(2)}) async-start(bf16[8,288,128]{2,1,0:T(8,128)(2,1)} %fusion.2), calls=%async_computation.1 | async-start | bytes 1179648 | tf_op jit(solution)/shard_map/all_to_all | solution.py:296
  37.2 3.0 %collective-permute-start = (bf16[8,512,128]{2,1,0:T(8,128)(2,1)}, bf16[8,512,128]{2,1,0:T(8,128)(2,1)S(1)}, u32[]{:S(2)}, u32[]{:S(2)}) collective-permute-start(bf16[8,512,128]{2,1,0:T(8,128)(2,1)} %slice.28), channel_id=1, source_target_pairs={{0,4},{4,0},{8,12},{12,8},{16,20},{20,16},{24,28},{28,24},{32,36},... | collective-permute-start | bytes 3145736 | tf_op jit(solution)/shard_map/ppermute | solution.py:317
  52.6 1.4 %copy-start = (bf16[17,256,256]{2,1,0:T(8,128)(2,1)}, bf16[17,256,256]{2,1,0:T(8,128)(2,1)S(1)}, u32[]{:S(2)}) copy-start(bf16[17,256,256]{2,1,0:T(8,128)(2,1)S(1)} %get-tuple-element.16.keys) | copy-start | bytes 6684676
  54.0 1.3 %copy-start.2 = (bf16[16,256,256]{2,1,0:T(8,128)(2,1)}, bf16[16,256,256]{2,1,0:T(8,128)(2,1)S(1)}, u32[]{:S(2)}) copy-start(bf16[16,256,256]{2,1,0:T(8,128)(2,1)S(1)} %get-tuple-element.18.values) | copy-start | bytes 6291460
  55.3 1.0 copy-start.4
  56.3 1.0 copy-start.6
  57.3 0.8 copy-start.8
  58.1 1.6 %copy-start.1 = (bf16[17,256,256]{2,1,0:T(8,128)(2,1)S(1)}, bf16[17,256,256]{2,1,0:T(8,128)(2,1)}, u32[]{:S(2)}) copy-start(bf16[17,256,256]{2,1,0:T(8,128)(2,1)} %copy-done) | copy-start | bytes 6684676
  59.7 1.6 %copy-start.3 = (bf16[16,256,256]{2,1,0:T(8,128)(2,1)S(1)}, bf16[16,256,256]{2,1,0:T(8,128)(2,1)}, u32[]{:S(2)}) copy-start(bf16[16,256,256]{2,1,0:T(8,128)(2,1)} %copy-done.2) | copy-start | bytes 6291460
  61.3 1.2 %copy-start.5 = (bf16[16,128,256]{2,1,0:T(8,128)(2,1)S(1)}, bf16[16,128,256]{2,1,0:T(8,128)(2,1)}, u32[]{:S(2)}) copy-start(bf16[16,128,256]{2,1,0:T(8,128)(2,1)} %copy-done.4) | copy-start | bytes 3145732
  62.5 1.2 %copy-start.7 = (bf16[8,256,256]{2,1,0:T(8,128)(2,1)S(1)}, bf16[8,256,256]{2,1,0:T(8,128)(2,1)}, u32[]{:S(2)}) copy-start(bf16[8,256,256]{2,1,0:T(8,128)(2,1)} %copy-done.6) | copy-start | bytes 3145732
  63.8 1.0 copy-start.9
  81.6 5.8 %collective-permute-start.1 = (bf16[8,512,128]{2,1,0:T(8,128)(2,1)}, bf16[8,512,128]{2,1,0:T(8,128)(2,1)}, u32[]{:S(2)}, u32[]{:S(2)}) collective-permute-start(bf16[8,512,128]{2,1,0:T(8,128)(2,1)} %get-tuple-element.24), channel_id=1, source_target_pairs={{0,4},{4,0},{8,12},{12,8},{16,20},{20,16},{24,28},{28,24},{32,36},... | collective-permute-start | bytes 3145736 | tf_op jit(solution)/shard_map/ppermute | solution.py:322
  81.9 16.0 %all-to-all-start.2 = ((bf16[8,256,128]{2,1,0:T(8,128)(2,1)}), bf16[8,256,128]{2,1,0:T(8,128)(2,1)S(1)}, u32[]{:S(2)}, u32[]{:S(2)}) async-start(bf16[8,256,128]{2,1,0:T(8,128)(2,1)} %get-tuple-element.22), calls=%async_computation.2 | async-start | bytes 1048576 | tf_op jit(solution)/shard_map/all_to_all | solution.py:296
  97.9 18.5 %all-to-all-start.3 = ((bf16[8,512,128]{2,1,0:T(8,128)(2,1)}), bf16[8,512,128]{2,1,0:T(8,128)(2,1)S(1)}, u32[]{:S(2)}, u32[]{:S(2)}) async-start(bf16[8,512,128]{2,1,0:T(8,128)(2,1)} %add_convert_fusion), calls=%async_computation.3 | async-start | bytes 2097152 | tf_op jit(solution)/shard_map/all_to_all | solution.py:296
where the time goes:
time: 120 us; the launch traced here: 119 us
  waiting for transfers between devices  41 us (34%)
  Pallas kernels  31.9 us (27%)
  local copies, waits for them, and re-layouts  18.9 us (16%)
  starting transfers between devices  18.2 us (15%)
  other arithmetic  7.68 us (6%)
    all_to_all x4, waiting for transfers between devices, exchange(): return lax.all_to_all(x, 'seq', 0, 0, axis_index_groups=groups)  39.1 us
    all_to_all x4, starting transfers between devices, exchange(): return lax.all_to_all(x, 'seq', 0, 0, axis_index_groups=groups)  17.9 us
    pallas_call x1, Pallas kernels, grads(): pl.pallas_call(grads_kernel, out_shape=(jax.ShapeDtypeStruct((chips, TILE...  16.8 us
    unnamed x31, local copies, waits for them, and re-layouts  16 us
    pallas_call x1, Pallas kernels, prepare(): pl.pallas_call(prepare_kernel, out_shape=(jax.ShapeDtypeStruct((blocks +...  12.4 us
    pallas_call x1, Pallas kernels, pack(): pl.pallas_call(pack_kernel, out_shape=jax.ShapeDtypeStruct((chips, 3 * ro...  2.68 us
    convert_element_type x1, other arithmetic, on_device(): dkv = exchange((keep + received.astype(jnp.float32)).astype(jnp.bfloat16))  2.42 us
  transfers between devices with their start and end apart: 6, of which 4 were waited for; matrix products, arithmetic and copies ran while one was open for 7% of the time, Pallas kernels for 10%

commit v1 on v0

v1 whole, which is shorter than its diff:
```python
import math

import jax
import jax.numpy as jnp
from jax import lax
from jax.experimental import pallas as pl
from jax.experimental.pallas import tpu as pltpu
from jax.sharding import PartitionSpec as P

HD = 128
QBLK = 128
CHUNK = 256
TILE = 2 * QBLK
GROUP = 3
SCALE = HD ** (-0.5)
RATE = SCALE * math.log2(math.e)
FLOOR = -1e30
EXTRA = 16

smem = pl.BlockSpec(memory_space=pltpu.SMEM)
vmem = pl.BlockSpec(memory_space=pltpu.VMEM)
params = pltpu.CompilerParams(vmem_limit_bytes=16 * 1024 * 1024)


def dot(a, b):
    return jnp.dot(a, b, preferred_element_type=jnp.float32)


def pack_kernel(ids_ref, k_ref, q_ref, out_ref):
    rows = k_ref.shape[0]
    heads = k_ref.shape[1] // HD
    line = lax.broadcasted_iota(jnp.int32, (EXTRA, HD), 0)
    note = jnp.where(line == 0, ids_ref[0], ids_ref[1]).astype(jnp.float32).astype(out_ref.dtype)
    for slot in range(out_ref.shape[0]):
        columns = slice(slot % heads * HD, (slot % heads + 1) * HD)
        out_ref[slot, :rows, :] = k_ref[:, columns]
        out_ref[slot, rows : 2 * rows, :] = q_ref[:, columns]
        out_ref[slot, 2 * rows :, :] = note


def pack(ids, k, q, chips):
    rows = k.shape[0]
    return pl.pallas_call(
        pack_kernel,
        out_shape=jax.ShapeDtypeStruct((chips, 2 * rows + EXTRA, HD), k.dtype),
        in_specs=[smem, vmem, vmem],
        out_specs=vmem,
        name="pack",
    )(ids, k, q)


def unpack_kernel(x_ref, *out_refs):
    rows, width = out_refs[0].shape
    for i, out_ref in enumerate(out_refs):
        for head in range(width // HD):
            columns = slice(head * HD, (head + 1) * HD)
            out_ref[:, columns] = x_ref[head, i * rows : (i + 1) * rows, :]


def unpack(x, rows, heads):
    number = x.shape[1] // rows
    return pl.pallas_call(
        unpack_kernel,
        out_shape=(jax.ShapeDtypeStruct((rows, heads * HD), x.dtype),) * number,
        in_specs=[vmem],
        out_specs=(vmem,) * number,
        name="unpack",
    )(x)


def place_key(keys, spot, k, edges):
    rows = lax.broadcasted_iota(jnp.int32, (CHUNK, HD), 0) + spot * CHUNK
    outside = (rows < edges[0:1]) | (rows >= edges[1:2])
    keys[spot, :, :HD] = k
    keys[spot, :, HD:] = jnp.where(outside, 1.0, 0.0).astype(jnp.bfloat16)


def place_query(qt, slot, q, token, sides):
    rows = slice(slot * QBLK, (slot + 1) * QBLK)
    tokens = lax.broadcasted_iota(jnp.int32, (EXTRA, QBLK), 1) + token
    within = (tokens >= sides[:EXTRA]) & (tokens < sides[EXTRA:])
    qt[:HD, rows] = q.T
    qt[HD : HD + EXTRA, rows] = jnp.where(within, FLOOR, 0.0).astype(jnp.bfloat16)


def block_rows(block, base, size):
    return pl.ds(pl.multiple_of(base + block % 2 * size, size), size)


def prepare_kernel(
    core_ref, order_ref, token_ref, count_ref, list_ref, first_ref, other_ref, edges, sides,
    level_ref,
    keys, qt, raw,
):
    core = core_ref[0]
    chips = first_ref.shape[0]
    tiles = level_ref.shape[0]

    def place(i, carry):
        place_key(keys, 2 * i + core, first_ref[i, :CHUNK, :], edges)
        place_key(keys, 2 * i + 1 - core, other_ref[i], edges)
        return carry

    lax.fori_loop(0, chips, place, 0)
    keys[2 * chips] = jnp.ones((CHUNK, 2 * HD), jnp.bfloat16)
    qt[HD:, :] = jnp.zeros((HD, TILE), jnp.bfloat16)

    def tile(t, carry):
        for slot in range(2):
            block = order_ref[2 * t + slot]
            q = first_ref[block // 2, block_rows(block, CHUNK, QBLK), :]
            place_query(qt, slot, q, token_ref[2 * t + slot], sides)
        steps = (count_ref[t] + GROUP - 1) // GROUP

        def score(i):
            i = jnp.minimum(i, steps - 1)
            for u in range(GROUP):
                raw[i % 2, u] = dot(keys[list_ref[t, GROUP * i + u]], qt[...])

        score(0)

        def totals(i, carry):
            top, total = carry
            s = raw[i % 2].reshape(GROUP * 4, 8, 8, TILE)
            new_top = jnp.maximum(top, jnp.max(jnp.max(s, axis=1), axis=0))
            added = jnp.sum(jnp.sum(jnp.exp2((s - new_top) * RATE), axis=1), axis=0)
            score(i + 1)
            return new_top, total * jnp.exp2((top - new_top) * RATE) + added

        top, total = lax.fori_loop(
            0, steps, totals,
            (jnp.full((8, TILE), FLOOR, jnp.float32), jnp.zeros((8, TILE), jnp.float32)),
        )
        row_top = jnp.max(top, axis=0, keepdims=True)
        row_sum = jnp.sum(total * jnp.exp2((top - row_top) * RATE), axis=0, keepdims=True)
        level_ref[t] = row_top + jnp.log2(row_sum) * (1.0 / RATE)
        return carry

    lax.fori_loop(0, tiles, tile, 0)


def prepare(scalars, first, other, edges, sides):
    chips = first.shape[0]
    blocks, tiles = 2 * chips, chips
    pairs = blocks * QBLK * 2048
    return pl.pallas_call(
        prepare_kernel,
        out_shape=jax.ShapeDtypeStruct((tiles, 1, TILE), jnp.float32),
        in_specs=[smem] * len(scalars) + [vmem] * 4,
        out_specs=vmem,
        scratch_shapes=[
            pltpu.VMEM((blocks + 1, CHUNK, 2 * HD), jnp.bfloat16),
            pltpu.VMEM((2 * HD, TILE), jnp.bfloat16),
            pltpu.VMEM((2, GROUP, CHUNK, TILE), jnp.float32),
        ],
        compiler_params=params,
        cost_estimate=pl.CostEstimate(
            flops=4 * pairs * HD, bytes_accessed=8 * 2**20, transcendentals=pairs
        ),
        name="prepare",
    )(*scalars, first, other, edges, sides)


def grads_kernel(
    core_ref, order_ref, token_ref, count_ref, list_ref, first_ref, other_ref, edges, sides,
    second_ref, second_other, level_ref,
    dq_ref, keep_ref, send_ref,
    keys, keys_t, values, qs, qt, gs, gt, acc_k, acc_v, acc_q,
):
    core = core_ref[0]
    chips = first_ref.shape[0]
    tiles = level_ref.shape[0]

    def place(i, carry):
        mine, theirs = 2 * i + core, 2 * i + 1 - core
        for spot, k, v in (
            (mine, first_ref[i, :CHUNK, :], second_ref[i, :CHUNK, :]),
            (theirs, other_ref[i], second_other[i]),
        ):
            place_key(keys, spot, k, edges)
            keys_t[spot] = k.T
            values[spot, :, :HD] = v
            values[spot, :, HD:] = jnp.full((CHUNK, HD), -1, jnp.bfloat16)
            acc_k[spot] = jnp.zeros((CHUNK, HD), jnp.float32)
            acc_v[spot] = jnp.zeros((CHUNK, HD), jnp.float32)
        return carry

    lax.fori_loop(0, chips, place, 0)
    qt[HD:, :] = jnp.zeros((HD, TILE), jnp.bfloat16)
    gt[HD:, :] = jnp.zeros((HD, TILE), jnp.bfloat16)

    def tile(t, carry):
        count = count_ref[t]
        blocks = [order_ref[2 * t + slot] for slot in range(2)]
        for slot, block in enumerate(blocks):
            rows = slice(slot * QBLK, (slot + 1) * QBLK)
            q = first_ref[block // 2, block_rows(block, CHUNK, QBLK), :]
            g = second_ref[block // 2, block_rows(block, CHUNK, QBLK), :]
            qs[rows, :] = q
            gs[rows, :] = g
            place_query(qt, slot, q, token_ref[2 * t + slot], sides)
            gt[:HD, rows] = g.T
            gt[HD : HD + EXTRA, rows] = second_ref[block // 2, block_rows(block, 2 * CHUNK, EXTRA), :]
        acc_q[...] = jnp.zeros_like(acc_q)
        level = level_ref[t]

        def some(first, number):
            spots = [list_ref[t, first + u] for u in range(number)]
            scores = [dot(keys[spot], qt[...]) for spot in spots]
            slopes = [dot(values[spot], gt[...]) for spot in spots]
            low = []
            for u, spot in enumerate(spots):
                p = jnp.exp2((scores[u] - level) * RATE)
                s = (p * slopes[u]).astype(jnp.bfloat16)
                acc_v[spot] += dot(p.astype(jnp.bfloat16), gs[...])
                acc_k[spot] += dot(s, qs[...])
                low.append(s)
            left = jnp.concatenate([keys_t[spot] for spot in spots], axis=1)
            acc_q[...] += dot(left, jnp.concatenate(low, axis=0))

        def step(i, carry):
            some(GROUP * i, GROUP)
            return carry

        full = count // GROUP
        lax.fori_loop(0, full, step, 0)
        for rest in range(1, GROUP):
            pl.when(count - GROUP * full == rest)(lambda: some(GROUP * full, rest))

        result = (acc_q[...] * SCALE).T.astype(jnp.bfloat16)
        for slot, block in enumerate(blocks):
            part = result[slot * QBLK : (slot + 1) * QBLK]
            dq_ref[block // 2, block_rows(block, 0, QBLK), :] = part
        return carry

    lax.fori_loop(0, tiles, tile, 0)

    def hand_out(i, carry):
        mine, theirs = 2 * i + core, 2 * i + 1 - core
        keep_ref[i, :CHUNK] = acc_k[mine] * SCALE
        keep_ref[i, CHUNK:] = acc_v[mine]
        send_ref[i, :CHUNK] = (acc_k[theirs] * SCALE).astype(jnp.bfloat16)
        send_ref[i, CHUNK:] = acc_v[theirs].astype(jnp.bfloat16)
        return carry

    lax.fori_loop(0, chips, hand_out, 0)


def grads(scalars, first, other, edges, sides, second, second_other, level):
    chips = second.shape[0]
    blocks = 2 * chips
    pairs = blocks * QBLK * 2048
    bf16 = jnp.bfloat16
    return pl.pallas_call(
        grads_kernel,
        out_shape=(
            jax.ShapeDtypeStruct((chips, TILE, HD), bf16),
            jax.ShapeDtypeStruct((chips, 2 * CHUNK, HD), jnp.float32),
            jax.ShapeDtypeStruct((chips, 2 * CHUNK, HD), bf16),
        ),
        in_specs=[smem] * len(scalars) + [vmem] * 7,
        out_specs=(vmem,) * 3,
        scratch_shapes=[
            pltpu.VMEM((blocks, CHUNK, 2 * HD), bf16),
            pltpu.VMEM((blocks, HD, CHUNK), bf16),
            pltpu.VMEM((blocks, CHUNK, 2 * HD), bf16),
            pltpu.VMEM((TILE, HD), bf16),
            pltpu.VMEM((2 * HD, TILE), bf16),
            pltpu.VMEM((TILE, HD), bf16),
            pltpu.VMEM((2 * HD, TILE), bf16),
            pltpu.VMEM((blocks, CHUNK, HD), jnp.float32),
            pltpu.VMEM((blocks, CHUNK, HD), jnp.float32),
            pltpu.VMEM((HD, TILE), jnp.float32),
        ],
        compiler_params=params,
        cost_estimate=pl.CostEstimate(
            flops=10 * pairs * HD, bytes_accessed=10 * 2**20, transcendentals=pairs
        ),
        name="grads",
    )(*scalars, first, other, edges, sides, second, second_other, level)


def plan(ids, lengths):
    blocks = ids.shape[0]
    ends = jnp.cumsum(lengths)
    offsets = ends - lengths
    place = jnp.arange(blocks, dtype=jnp.int32)
    rank = jnp.sum((ids[None, :] < ids[:, None]).astype(jnp.int32), axis=1)
    hit = (rank[None, :] == place[:, None]).astype(jnp.int32)
    order = jnp.sum(hit * place[None, :], axis=1)
    tokens = jnp.sum(hit * ids[None, :], axis=1) * QBLK

    def bounds(token):
        inside = (token[:, None] >= offsets) & (token[:, None] < ends)
        return [jnp.sum(jnp.where(inside, x, 0), axis=1) for x in (offsets, ends)]

    first = bounds(tokens)[0] // CHUNK
    last = (bounds(tokens + QBLK - 1)[1] - 1) // CHUNK
    needed = (place[None, :] >= first[:, None]) & (place[None, :] <= last[:, None])
    needed = (needed[0::2] | needed[1::2]).astype(jnp.int32)
    count = jnp.sum(needed, axis=1)
    before = jnp.sum(needed[:, None, :] * (place[None, :] < place[:, None]), axis=2)
    slots = jnp.arange(blocks + GROUP, dtype=jnp.int32)
    chosen = (before[:, None, :] == slots[None, :, None]) & (needed[:, None, :] > 0)
    chunk_list = jnp.sum(jnp.where(chosen, place[None, None, :], 0), axis=2)
    chunk_list = jnp.where(slots[None, :] < count[:, None], chunk_list, blocks)
    return order, tokens, count, chunk_list


def edges_of(lengths, tokens):
    ends = jnp.cumsum(lengths)
    offsets = ends - lengths
    spare = HD - lengths.shape[0]
    edges = jnp.stack([jnp.pad(offsets, (0, spare)), jnp.pad(ends, (0, spare), constant_values=tokens)])
    spare = EXTRA - lengths.shape[0]
    sides = [jnp.pad(x, (0, spare), constant_values=tokens) for x in (offsets, ends)]
    return edges, jnp.broadcast_to(jnp.concatenate(sides)[:, None], (2 * EXTRA, QBLK))


def split_in_three(x):
    parts = []
    for _ in range(3):
        part = lax.reduce_precision(x, exponent_bits=8, mantissa_bits=7)
        parts.append(part.astype(jnp.bfloat16))
        x = x - part
    return jnp.stack(parts, axis=-2)


def on_device(queries, keys_in, values_in, forward_out, grad_out, lengths, query_block):
    size = lax.axis_size("seq")
    chips = size // 2
    core = lax.axis_index("seq") % 2
    rows = queries.shape[0]
    heads = queries.shape[1] // HD
    groups = [[2 * i + c for i in range(chips)] for c in range(2)]
    swap = [(i, i ^ 1) for i in range(size)]

    def exchange(x):
        return lax.all_to_all(x, "seq", 0, 0, axis_index_groups=groups)

    first = exchange(pack(query_block, keys_in, queries, chips))

    delta = jnp.sum(
        (grad_out.astype(jnp.float32) * forward_out.astype(jnp.float32)).reshape(rows, heads, HD),
        axis=2,
    )
    parts = split_in_three(delta.T.reshape(heads, rows // QBLK, QBLK))
    parts = jnp.pad(parts, ((0, 0), (0, 0), (0, EXTRA - 3), (0, 0))).reshape(heads, -1, HD)
    by_head = [x.reshape(rows, heads, HD).transpose(1, 0, 2) for x in (values_in, grad_out)]
    second = jnp.concatenate(by_head + [parts], axis=1)
    second = jnp.pad(second, ((0, chips - heads), (0, 0), (0, 0)))
    first, second = lax.optimization_barrier((first, second))
    second = exchange(second)

    ids = first[:, 2 * rows : 2 * rows + 2, 0].astype(jnp.int32).reshape(-1)
    scalars = (jnp.full((1,), core, jnp.int32), *plan(ids, lengths))
    edges, sides = edges_of(lengths, size * rows)
    other = lax.ppermute(first[:, :rows], "seq", swap)
    level = prepare(scalars, first, other, edges, sides)
    second, level = lax.optimization_barrier((second, level))
    second_other = lax.ppermute(second[:, :rows], "seq", swap)
    dq, keep, send = grads(
        scalars, first, other, edges, sides, second, second_other, level
    )

    received = lax.ppermute(send, "seq", swap)
    dkv = (keep + received.astype(jnp.float32)).astype(jnp.bfloat16)
    return unpack(exchange(jnp.concatenate([dq, dkv], axis=1)), rows, heads)


def solution(mesh):
    spec = P(("win", "seq"), "head")
    in_specs = (spec,) * 5 + (P("win"), P(("win", "seq")))
    return jax.shard_map(
        on_device, mesh=mesh, in_specs=in_specs, out_specs=(spec,) * 3, check_vma=False
    )
```

time: 120 us -> 96.1 us (0.80)
  blocking collectives: 0 us -> 25.8 us
  waiting for transfers between devices: 41 us -> 20.4 us
  local copies, waits for them, and re-layouts: 18.9 us -> 1.44 us
  starting transfers between devices: 18.2 us -> 9.06 us
  other arithmetic: 7.68 us -> 3.14 us
  Pallas kernels: 31.9 us -> 34.8 us
    all_to_all x0 -> x1, blocking collectives: none -> 25.8 us  [exchange(): return lax.all_to_all(x, 'seq', 0, 0, axis_index_groups=groups)]
    all_to_all x4 -> x2, waiting for transfers between devices: 39.1 us -> 14.5 us  [exchange(): return lax.all_to_all(x, 'seq', 0, 0, axis_index_groups=groups)]
    unnamed x31 -> x11, local copies, waits for them, and re-layouts: 16 us -> 0.68 us
    all_to_all x4 -> x2, starting transfers between devices: 17.9 us -> 8.81 us  [exchange(): return lax.all_to_all(x, 'seq', 0, 0, axis_index_groups=groups)]
    convert_element_type x5 -> x2, other arithmetic: 4.33 us -> 0.48 us  [the longest x1 0.27 us: on_device(): dkv = (keep + received.astype(jnp.float32)).astype(jnp.bfloat16)]
    ppermute x1, waiting for transfers between devices: 0.01 us -> 2.65 us  [on_device(): received = lax.ppermute(send, 'seq', swap)]
    pallas_call x2 -> x3, Pallas kernels: 15.1 us -> 17.4 us  [the longest x1 12.4 us: prepare(): pl.pallas_call(prepare_kernel, out_shape=jax.ShapeDtypeStruct((tiles, 1,...]
    ppermute x1 -> x2, waiting for transfers between devices: 1.9 us -> 3.25 us  [the longest x1 1.9 us: on_device(): second_other = lax.ppermute(second[:, :rows], 'seq', swap)]
  transfers between devices with their start and end apart: 6 -> 5, of which waited for: 4 -> 5; matrix products, arithmetic and copies ran while one was open for 7% -> 3% of each run, Pallas kernels for 10% -> 13%
where the time goes in v1:
time: 96.1 us; the launch traced here: 95.6 us
  Pallas kernels  34.8 us (36%)
  blocking collectives  25.8 us (27%)
  waiting for transfers between devices  20.4 us (21%)
  starting transfers between devices  9.06 us (9%)
  other arithmetic  3.14 us (3%)
  local copies, waits for them, and re-layouts  1.44 us (1%)
    all_to_all x1, blocking collectives, exchange(): return lax.all_to_all(x, 'seq', 0, 0, axis_index_groups=groups)  25.8 us
    pallas_call x1, Pallas kernels, grads(): pl.pallas_call(grads_kernel, out_shape=(jax.ShapeDtypeStruct((chips, TILE...  17.4 us
    all_to_all x2, waiting for transfers between devices, exchange(): return lax.all_to_all(x, 'seq', 0, 0, axis_index_groups=groups)  14.5 us
    pallas_call x1, Pallas kernels, prepare(): pl.pallas_call(prepare_kernel, out_shape=jax.ShapeDtypeStruct((tiles, 1,...  12.4 us
    all_to_all x2, starting transfers between devices, exchange(): return lax.all_to_all(x, 'seq', 0, 0, axis_index_groups=groups)  8.81 us
    ppermute x1, waiting for transfers between devices, on_device(): received = lax.ppermute(send, 'seq', swap)  2.65 us
    pallas_call x1, Pallas kernels, unpack(): pl.pallas_call(unpack_kernel, out_shape=(jax.ShapeDtypeStruct((rows, head...  2.61 us
    pallas_call x1, Pallas kernels, pack(): pl.pallas_call(pack_kernel, out_shape=jax.ShapeDtypeStruct((chips, 2 * ro...  2.39 us
  transfers between devices with their start and end apart: 5, of which 5 were waited for; matrix products, arithmetic and copies ran while one was open for 3% of the time, Pallas kernels for 13%

profile of v1, /device:TPU:4, one launch (start us, length us, event | category | flops | bytes accessed | tf_op | source)
XLA Modules:
  0.0 95.6 jit_solution(11311818144820206944)
XLA Ops:
  0.7 2.4 %pack.1 = bf16[8,528,128]{2,1,0:T(8,128)(2,1)} custom-call(s32[2]{0:T(128)} %ids_ref.1, bf16[256,768]{1,0:T(8,128)(2,1)} %k_ref.1, bf16[256,768]{1,0:T(8,128)(2,1)} %q_ref.1), custom_call_target="tpu_custom_call" | custom-call | tf_op jit(solution)/shard_map/pack/pallas_call | solution.py:43
  3.0 5.2 %all-to-all-start = ((bf16[8,528,128]{2,1,0:T(8,128)(2,1)}), bf16[8,528,128]{2,1,0:T(8,128)(2,1)S(1)}, u32[]{:S(2)}, u32[]{:S(2)}) async-start(bf16[8,528,128]{2,1,0:T(8,128)(2,1)} %pack.1), calls=%async_computation | async-start | bytes 2162688 | tf_op jit(solution)/shard_map/all_to_all | solution.py:339
  8.3 0.2 reduce-window.8
  8.5 0.2 copy.18
  8.7 0.2 copy.19
  8.9 0.2 copy.16
  9.1 0.2 copy.17
  9.3 0.2 copy-done.2
  9.5 0.2 copy.21
  10.0 1.1 %fusion.4 = bf16[8,544,128]{2,1,0:T(8,128)(2,1)} fusion(bf16[6,32,128]{2,1,0:T(8,128)(2,1)S(1)} %bitcast.20, bf16[6,256,128]{2,1,0:T(8,128)(2,1)S(1)} %bitcast.18, bf16[6,256,128]{2,1,0:T(8,128)(2,1)S(1)} %bitcast.19), kind=kLoop, calls=%fused_computation.7 | loop fusion | flops 5570560 | bytes 1949696 | tf_op jit(solution)/shard_map/concatenate | solution.py:350
  11.1 13.3 %all-to-all-done.first_ref = bf16[8,528,128]{2,1,0:T(8,128)(2,1)S(1)} async-done(((bf16[8,528,128]{2,1,0:T(8,128)(2,1)}), bf16[8,528,128]{2,1,0:T(8,128)(2,1)S(1)}, u32[]{:S(2)}, u32[]{:S(2)}) %all-to-all-start) | async-done | bytes 1081376 | tf_op jit(solution)/shard_map/all_to_all | solution.py:339
  24.3 0.2 convert_reduce_fusion
  24.6 0.2 convert_reduce_fusion.1
  24.8 0.1 select_reduce_fusion.1
  24.9 0.1 select_reduce_fusion.4
  25.2 3.6 %all-to-all-start.1 = ((bf16[8,544,128]{2,1,0:T(8,128)(2,1)}), bf16[8,544,128]{2,1,0:T(8,128)(2,1)S(1)}, u32[]{:S(2)}, u32[]{:S(2)}) async-start(bf16[8,544,128]{2,1,0:T(8,128)(2,1)} %fusion.4), calls=%async_computation.1 | async-start | bytes 2228224 | tf_op jit(solution)/shard_map/all_to_all | solution.py:339
  28.8 0.1 collective-permute-start
  28.9 0.1 fusion.16.count_ref
  29.0 0.2 multiply_reduce_fusion
  29.2 0.1 select_reduce_fusion
  29.4 1.4 %collective-permute-done.other_ref = bf16[8,256,128]{2,1,0:T(8,128)(2,1)S(1)} collective-permute-done((bf16[8,256,128]{2,1,0:T(8,128)(2,1)S(1)}, bf16[8,256,128]{2,1,0:T(8,128)(2,1)S(1)}, u32[]{:S(2)}, u32[]{:S(2)}) %collective-permute-start) | collective-permute-done | bytes 524320 | tf_op jit(solution)/shard_map/ppermute | solution.py:358
  30.9 12.4 %prepare.1.level_ref = f32[8,1,256]{2,1,0:T(1,128)S(1)} custom-call(s32[1]{0:T(128)} %bitcast.core_ref, s32[16]{0:T(128)S(1)} %get-tuple-element.20.order_ref, s32[16]{0:T(128)S(1)} %get-tuple-element.27.token_ref, s32[8]{0:T(128)S(1)} %fusion.16.count_ref, s32[8,19]{1,0:T(8,128)S(1)} %fusion.15.list_ref, bf16[8,528,128]{2,1,0:T(8,128)(2,1)S(1)} %all-to-all-done.first_ref, ...), custom_call_target="tpu_custom_call" | custom-call | flops 2147483648 | bytes 8388608 | tf_op jit(solution)/shard_map/prepare/pallas_call | solution.py:146
  43.3 1.3 %all-to-all-done.1.second_ref = bf16[8,544,128]{2,1,0:T(8,128)(2,1)S(1)} async-done(((bf16[8,544,128]{2,1,0:T(8,128)(2,1)}), bf16[8,544,128]{2,1,0:T(8,128)(2,1)S(1)}, u32[]{:S(2)}, u32[]{:S(2)}) %all-to-all-start.1) | async-done | bytes 1114144 | tf_op jit(solution)/shard_map/all_to_all | solution.py:339
  44.6 0.1 collective-permute-start.1
  44.7 1.9 %collective-permute-done.1.second_other = bf16[8,256,128]{2,1,0:T(8,128)(2,1)S(1)} collective-permute-done((bf16[8,256,128]{2,1,0:T(8,128)(2,1)S(1)}, bf16[8,256,128]{2,1,0:T(8,128)(2,1)S(1)}, u32[]{:S(2)}, u32[]{:S(2)}) %collective-permute-start.1) | collective-permute-done | bytes 524320 | tf_op jit(solution)/shard_map/ppermute | solution.py:361
  46.6 17.4 %grads.1 = (bf16[8,256,128]{2,1,0:T(8,128)(2,1)S(1)}, f32[8,512,128]{2,1,0:T(8,128)S(1)}, bf16[8,512,128]{2,1,0:T(8,128)(2,1)S(1)}) custom-call(s32[1]{0:T(128)} %bitcast.core_ref, s32[16]{0:T(128)S(1)} %get-tuple-element.20.order_ref, s32[16]{0:T(128)S(1)} %get-tuple-element.27.token_ref, s32[8]{0:T(128)S(1)} %fusion.16.count_ref, ...), custom_call_target="tpu_custom_call" | custom-call | flops 5368709120 | bytes 10485760 | tf_op jit(solution)/shard_map/grads/pallas_call | solution.py:254
  64.0 0.1 collective-permute-start.2
  64.1 2.6 %collective-permute-done.2 = bf16[8,512,128]{2,1,0:T(8,128)(2,1)S(1)} collective-permute-done((bf16[8,512,128]{2,1,0:T(8,128)(2,1)S(1)}, bf16[8,512,128]{2,1,0:T(8,128)(2,1)S(1)}, u32[]{:S(2)}, u32[]{:S(2)}) %collective-permute-start.2) | collective-permute-done | bytes 1048608 | tf_op jit(solution)/shard_map/ppermute | solution.py:366
  66.8 0.3 add_convert_fusion
  67.0 0.1 pad_maximum_fusion
  67.2 25.8 %all_to_all.15.x_ref = bf16[8,768,128]{2,1,0:T(8,128)(2,1)} all-to-all(bf16[8,768,128]{2,1,0:T(8,128)(2,1)S(1)} %pad_maximum_fusion), channel_id=1, replica_groups={{0,8,16,24,32,40,48,56},{4,12,20,28,36,44,52,60},{1,9,17,25,33,41,49,57..., dimensions={0} | all-to-all | bytes 3145728 | tf_op jit(solution)/shard_map/all_to_all | solution.py:339
  93.0 2.6 %unpack.1 = (bf16[256,768]{1,0:T(8,128)(2,1)}, bf16[256,768]{1,0:T(8,128)(2,1)}, bf16[256,768]{1,0:T(8,128)(2,1)}) custom-call(bf16[8,768,128]{2,1,0:T(8,128)(2,1)} %all_to_all.15.x_ref), custom_call_target="tpu_custom_call" | custom-call | tf_op jit(solution)/shard_map/unpack/pallas_call | solution.py:62
  (28 shorter events, 0.8 us)
Async XLA Ops:
  0.6 7.7 %copy-start.3 = (s32[8]{0:T(128)S(1)}, s32[8]{0:T(128)}, u32[]{:S(2)}) copy-start(s32[8]{0:T(128)} %param.12) | copy-start | bytes 100
  0.6 7.8 %copy-start = (bf16[256,768]{1,0:T(8,128)(2,1)S(1)}, bf16[256,768]{1,0:T(8,128)(2,1)}, u32[]{:S(2)}) copy-start(bf16[256,768]{1,0:T(8,128)(2,1)} %param.11) | copy-start | bytes 1179652
  3.0 5.9 %copy-start.1 = (bf16[256,768]{1,0:T(8,128)(2,1)S(1)}, bf16[256,768]{1,0:T(8,128)(2,1)}, u32[]{:S(2)}) copy-start(bf16[256,768]{1,0:T(8,128)(2,1)} %param.9) | copy-start | bytes 1179652
  3.0 21.3 %all-to-all-start = ((bf16[8,528,128]{2,1,0:T(8,128)(2,1)}), bf16[8,528,128]{2,1,0:T(8,128)(2,1)S(1)}, u32[]{:S(2)}, u32[]{:S(2)}) async-start(bf16[8,528,128]{2,1,0:T(8,128)(2,1)} %pack.1), calls=%async_computation | async-start | bytes 2162688 | tf_op jit(solution)/shard_map/all_to_all | solution.py:339
  8.5 1.0 %copy-start.2 = (bf16[256,768]{1,0:T(8,128)(2,1)S(1)}, bf16[256,768]{1,0:T(8,128)(2,1)}, u32[]{:S(2)}) copy-start(bf16[256,768]{1,0:T(8,128)(2,1)} %param.10) | copy-start | bytes 1179652
  25.2 19.3 %all-to-all-start.1 = ((bf16[8,544,128]{2,1,0:T(8,128)(2,1)}), bf16[8,544,128]{2,1,0:T(8,128)(2,1)S(1)}, u32[]{:S(2)}, u32[]{:S(2)}) async-start(bf16[8,544,128]{2,1,0:T(8,128)(2,1)} %fusion.4), calls=%async_computation.1 | async-start | bytes 2228224 | tf_op jit(solution)/shard_map/all_to_all | solution.py:339
  28.8 2.0 %collective-permute-start = (bf16[8,256,128]{2,1,0:T(8,128)(2,1)S(1)}, bf16[8,256,128]{2,1,0:T(8,128)(2,1)S(1)}, u32[]{:S(2)}, u32[]{:S(2)}) collective-permute-start(bf16[8,256,128]{2,1,0:T(8,128)(2,1)S(1)} %slice.18), channel_id=1, source_target_pairs={{0,4},{4,0},{8,12},{12,8},{16,20},{20,16},{24,28},{28,24},{32,36},... | collective-permute-start | bytes 1572872 | tf_op jit(solution)/shard_map/ppermute | solution.py:358
  44.6 2.0 %collective-permute-start.1 = (bf16[8,256,128]{2,1,0:T(8,128)(2,1)S(1)}, bf16[8,256,128]{2,1,0:T(8,128)(2,1)S(1)}, u32[]{:S(2)}, u32[]{:S(2)}) collective-permute-start(bf16[8,256,128]{2,1,0:T(8,128)(2,1)S(1)} %slice.19), channel_id=1, source_target_pairs={{0,4},{4,0},{8,12},{12,8},{16,20},{20,16},{24,28},{28,24},{32,36},... | collective-permute-start | bytes 1572872 | tf_op jit(solution)/shard_map/ppermute | solution.py:361
  64.0 2.7 %collective-permute-start.2 = (bf16[8,512,128]{2,1,0:T(8,128)(2,1)S(1)}, bf16[8,512,128]{2,1,0:T(8,128)(2,1)S(1)}, u32[]{:S(2)}, u32[]{:S(2)}) collective-permute-start(bf16[8,512,128]{2,1,0:T(8,128)(2,1)S(1)} %get-tuple-element.16), channel_id=1, source_target_pairs={{0,4},{4,0},{8,12},{12,8},{16,20},{20,16},{24,28},{28,24},{32,36},... | collective-permute-start | bytes 3145736 | tf_op jit(solution)/shard_map/ppermute | solution.py:366

commit v2 on v1

--- a/solution.py
+++ b/solution.py
@@ -11,7 +11,7 @@
 QBLK = 128
 CHUNK = 256
 TILE = 2 * QBLK
-GROUP = 3
+GROUP = 4
 SCALE = HD ** (-0.5)
 RATE = SCALE * math.log2(math.e)
 FLOOR = -1e30
@@ -19,7 +19,7 @@
 
 smem = pl.BlockSpec(memory_space=pltpu.SMEM)
 vmem = pl.BlockSpec(memory_space=pltpu.VMEM)
-params = pltpu.CompilerParams(vmem_limit_bytes=16 * 1024 * 1024)
+params = pltpu.CompilerParams(vmem_limit_bytes=32 * 1024 * 1024)
 
 
 def dot(a, b):
@@ -88,9 +88,9 @@
 
 
 def prepare_kernel(
-    core_ref, order_ref, token_ref, count_ref, list_ref, first_ref, other_ref, edges, sides,
+    core_ref, order_ref, token_ref, steps_ref, tile_ref, spot_ref, first_ref, other_ref, edges, sides,
     level_ref,
-    keys, qt, raw,
+    keys, qt, raw, tops, totals,
 ):
     core = core_ref[0]
     chips = first_ref.shape[0]
@@ -99,44 +99,47 @@
     def place(i, carry):
         place_key(keys, 2 * i + core, first_ref[i, :CHUNK, :], edges)
         place_key(keys, 2 * i + 1 - core, other_ref[i], edges)
+        for slot in range(2):
+            block = order_ref[2 * i + slot]
+            q = first_ref[block // 2, block_rows(block, CHUNK, QBLK), :]
+            place_query(qt.at[i], slot, q, token_ref[2 * i + slot], sides)
+        qt[i, HD + EXTRA :, :] = jnp.zeros((HD - EXTRA, TILE), jnp.bfloat16)
+        tops[i] = jnp.full((8, TILE), FLOOR, jnp.float32)
+        totals[i] = jnp.zeros((8, TILE), jnp.float32)
         return carry
 
     lax.fori_loop(0, chips, place, 0)
     keys[2 * chips] = jnp.ones((CHUNK, 2 * HD), jnp.bfloat16)
-    qt[HD:, :] = jnp.zeros((HD, TILE), jnp.bfloat16)
-
-    def tile(t, carry):
-        for slot in range(2):
-            block = order_ref[2 * t + slot]
-            q = first_ref[block // 2, block_rows(block, CHUNK, QBLK), :]
-            place_query(qt, slot, q, token_ref[2 * t + slot], sides)
-        steps = (count_ref[t] + GROUP - 1) // GROUP
-
-        def score(i):
-            i = jnp.minimum(i, steps - 1)
-            for u in range(GROUP):
-                raw[i % 2, u] = dot(keys[list_ref[t, GROUP * i + u]], qt[...])
-
-        score(0)
-
-        def totals(i, carry):
-            top, total = carry
-            s = raw[i % 2].reshape(GROUP * 4, 8, 8, TILE)
-            new_top = jnp.maximum(top, jnp.max(jnp.max(s, axis=1), axis=0))
-            added = jnp.sum(jnp.sum(jnp.exp2((s - new_top) * RATE), axis=1), axis=0)
-            score(i + 1)
-            return new_top, total * jnp.exp2((top - new_top) * RATE) + added
-
-        top, total = lax.fori_loop(
-            0, steps, totals,
-            (jnp.full((8, TILE), FLOOR, jnp.float32), jnp.zeros((8, TILE), jnp.float32)),
-        )
+
+    def score(i, u):
+        return dot(keys[spot_ref[GROUP * i + u]], qt[tile_ref[GROUP * i + u]])
+
+    for u in range(GROUP):
+        raw[0, u] = score(0, u)
+
+    def step(i, carry):
+        parts = []
+        for u in range(GROUP):
+            s = raw[i % 2, u].reshape(4, 8, 8, TILE)
+            top = jnp.max(jnp.max(s, axis=1), axis=0)
+            total = jnp.sum(jnp.sum(jnp.exp2((s - top) * RATE), axis=1), axis=0)
+            parts.append((top, total))
+        for u in range(GROUP):
+            raw[(i + 1) % 2, u] = score(i + 1, u)
+        for u, (top, total) in enumerate(parts):
+            t = tile_ref[GROUP * i + u]
+            old = tops[t]
+            new = jnp.maximum(old, top)
+            totals[t] = totals[t] * jnp.exp2((old - new) * RATE) + total * jnp.exp2((top - new) * RATE)
+            tops[t] = new
+        return carry
+
+    lax.fori_loop(0, steps_ref[0], step, 0)
+    for t in range(tiles):
+        top = tops[t]
         row_top = jnp.max(top, axis=0, keepdims=True)
-        row_sum = jnp.sum(total * jnp.exp2((top - row_top) * RATE), axis=0, keepdims=True)
+        row_sum = jnp.sum(totals[t] * jnp.exp2((top - row_top) * RATE), axis=0, keepdims=True)
         level_ref[t] = row_top + jnp.log2(row_sum) * (1.0 / RATE)
-        return carry
-
-    lax.fori_loop(0, tiles, tile, 0)
 
 
 def prepare(scalars, first, other, edges, sides):
@@ -150,8 +153,10 @@
         out_specs=vmem,
         scratch_shapes=[
             pltpu.VMEM((blocks + 1, CHUNK, 2 * HD), jnp.bfloat16),
-            pltpu.VMEM((2 * HD, TILE), jnp.bfloat16),
+            pltpu.VMEM((tiles, 2 * HD, TILE), jnp.bfloat16),
             pltpu.VMEM((2, GROUP, CHUNK, TILE), jnp.float32),
+            pltpu.VMEM((tiles, 8, TILE), jnp.float32),
+            pltpu.VMEM((tiles, 8, TILE), jnp.float32),
         ],
         compiler_params=params,
         cost_estimate=pl.CostEstimate(
@@ -162,10 +167,10 @@
 
 
 def grads_kernel(
-    core_ref, order_ref, token_ref, count_ref, list_ref, first_ref, other_ref, edges, sides,
+    core_ref, order_ref, token_ref, steps_ref, tile_ref, spot_ref, first_ref, other_ref, edges, sides,
     second_ref, second_other, level_ref,
     dq_ref, keep_ref, send_ref,
-    keys, keys_t, values, qs, qt, gs, gt, acc_k, acc_v, acc_q,
+    keys, keys_t, values, qs, qt, gs, gt, raw, slope, acc_k, acc_v, acc_q,
 ):
     core = core_ref[0]
     chips = first_ref.shape[0]
@@ -183,57 +188,53 @@
             values[spot, :, HD:] = jnp.full((CHUNK, HD), -1, jnp.bfloat16)
             acc_k[spot] = jnp.zeros((CHUNK, HD), jnp.float32)
             acc_v[spot] = jnp.zeros((CHUNK, HD), jnp.float32)
-        return carry
-
-    lax.fori_loop(0, chips, place, 0)
-    qt[HD:, :] = jnp.zeros((HD, TILE), jnp.bfloat16)
-    gt[HD:, :] = jnp.zeros((HD, TILE), jnp.bfloat16)
-
-    def tile(t, carry):
-        count = count_ref[t]
-        blocks = [order_ref[2 * t + slot] for slot in range(2)]
-        for slot, block in enumerate(blocks):
+        acc_q[i] = jnp.zeros((HD, TILE), jnp.float32)
+        for slot in range(2):
+            block = order_ref[2 * i + slot]
             rows = slice(slot * QBLK, (slot + 1) * QBLK)
             q = first_ref[block // 2, block_rows(block, CHUNK, QBLK), :]
             g = second_ref[block // 2, block_rows(block, CHUNK, QBLK), :]
-            qs[rows, :] = q
-            gs[rows, :] = g
-            place_query(qt, slot, q, token_ref[2 * t + slot], sides)
-            gt[:HD, rows] = g.T
-            gt[HD : HD + EXTRA, rows] = second_ref[block // 2, block_rows(block, 2 * CHUNK, EXTRA), :]
-        acc_q[...] = jnp.zeros_like(acc_q)
-        level = level_ref[t]
-
-        def some(first, number):
-            spots = [list_ref[t, first + u] for u in range(number)]
-            scores = [dot(keys[spot], qt[...]) for spot in spots]
-            slopes = [dot(values[spot], gt[...]) for spot in spots]
-            low = []
-            for u, spot in enumerate(spots):
-                p = jnp.exp2((scores[u] - level) * RATE)
-                s = (p * slopes[u]).astype(jnp.bfloat16)
-                acc_v[spot] += dot(p.astype(jnp.bfloat16), gs[...])
-                acc_k[spot] += dot(s, qs[...])
-                low.append(s)
-            left = jnp.concatenate([keys_t[spot] for spot in spots], axis=1)
-            acc_q[...] += dot(left, jnp.concatenate(low, axis=0))
-
-        def step(i, carry):
-            some(GROUP * i, GROUP)
-            return carry
-
-        full = count // GROUP
-        lax.fori_loop(0, full, step, 0)
-        for rest in range(1, GROUP):
-            pl.when(count - GROUP * full == rest)(lambda: some(GROUP * full, rest))
-
-        result = (acc_q[...] * SCALE).T.astype(jnp.bfloat16)
-        for slot, block in enumerate(blocks):
-            part = result[slot * QBLK : (slot + 1) * QBLK]
-            dq_ref[block // 2, block_rows(block, 0, QBLK), :] = part
-        return carry
-
-    lax.fori_loop(0, tiles, tile, 0)
+            qs[i, rows, :] = q
+            gs[i, rows, :] = g
+            place_query(qt.at[i], slot, q, token_ref[2 * i + slot], sides)
+            gt[i, :HD, rows] = g.T
+            delta = second_ref[block // 2, block_rows(block, 2 * CHUNK, EXTRA), :]
+            gt[i, HD : HD + EXTRA, rows] = delta
+        for ref in (qt, gt):
+            ref[i, HD + EXTRA :, :] = jnp.zeros((HD - EXTRA, TILE), jnp.bfloat16)
+        return carry
+
+    lax.fori_loop(0, chips, place, 0)
+    none = 2 * chips
+    keys[none] = jnp.ones((CHUNK, 2 * HD), jnp.bfloat16)
+    keys_t[none] = jnp.zeros((HD, CHUNK), jnp.bfloat16)
+    values[none] = jnp.zeros((CHUNK, 2 * HD), jnp.bfloat16)
+    acc_k[none] = jnp.zeros((CHUNK, HD), jnp.float32)
+    acc_v[none] = jnp.zeros((CHUNK, HD), jnp.float32)
+
+    def unit(i, u):
+        return tile_ref[GROUP * i + u], spot_ref[GROUP * i + u]
+
+    def ahead(i):
+        for u in range(GROUP):
+            t, spot = unit(i, u)
+            raw[i % 2, u] = dot(keys[spot], qt[t])
+            slope[i % 2, u] = dot(values[spot], gt[t])
+
+    ahead(0)
+
+    def step(i, carry):
+        for u in range(GROUP):
+            t, spot = unit(i, u)
+            p = jnp.exp2((raw[i % 2, u] - level_ref[t]) * RATE)
+            s = (p * slope[i % 2, u]).astype(jnp.bfloat16)
+            acc_v[spot] += dot(p.astype(jnp.bfloat16), gs[t])
+            acc_k[spot] += dot(s, qs[t])
+            acc_q[t] += dot(keys_t[spot], s)
+        ahead(i + 1)
+        return carry
+
+    lax.fori_loop(0, steps_ref[0], step, 0)
 
     def hand_out(i, carry):
         mine, theirs = 2 * i + core, 2 * i + 1 - core
@@ -241,6 +242,11 @@
         keep_ref[i, CHUNK:] = acc_v[mine]
         send_ref[i, :CHUNK] = (acc_k[theirs] * SCALE).astype(jnp.bfloat16)
         send_ref[i, CHUNK:] = acc_v[theirs].astype(jnp.bfloat16)
+        result = (acc_q[i] * SCALE).T.astype(jnp.bfloat16)
+        for slot in range(2):
+            block = order_ref[2 * i + slot]
+            part = result[slot * QBLK : (slot + 1) * QBLK]
+            dq_ref[block // 2, block_rows(block, 0, QBLK), :] = part
         return carry
 
     lax.fori_loop(0, chips, hand_out, 0)
@@ -248,29 +254,31 @@
 
 def grads(scalars, first, other, edges, sides, second, second_other, level):
     chips = second.shape[0]
-    blocks = 2 * chips
+    blocks, tiles = 2 * chips, chips
     pairs = blocks * QBLK * 2048
-    bf16 = jnp.bfloat16
+    bf16, f32 = jnp.bfloat16, jnp.float32
     return pl.pallas_call(
         grads_kernel,
         out_shape=(
             jax.ShapeDtypeStruct((chips, TILE, HD), bf16),
-            jax.ShapeDtypeStruct((chips, 2 * CHUNK, HD), jnp.float32),
+            jax.ShapeDtypeStruct((chips, 2 * CHUNK, HD), f32),
             jax.ShapeDtypeStruct((chips, 2 * CHUNK, HD), bf16),
         ),
         in_specs=[smem] * len(scalars) + [vmem] * 7,
         out_specs=(vmem,) * 3,
         scratch_shapes=[
-            pltpu.VMEM((blocks, CHUNK, 2 * HD), bf16),
-            pltpu.VMEM((blocks, HD, CHUNK), bf16),
-            pltpu.VMEM((blocks, CHUNK, 2 * HD), bf16),
-            pltpu.VMEM((TILE, HD), bf16),
-            pltpu.VMEM((2 * HD, TILE), bf16),
-            pltpu.VMEM((TILE, HD), bf16),
-            pltpu.VMEM((2 * HD, TILE), bf16),
-            pltpu.VMEM((blocks, CHUNK, HD), jnp.float32),
-            pltpu.VMEM((blocks, CHUNK, HD), jnp.float32),
-            pltpu.VMEM((HD, TILE), jnp.float32),
+            pltpu.VMEM((blocks + 1, CHUNK, 2 * HD), bf16),
+            pltpu.VMEM((blocks + 1, HD, CHUNK), bf16),
+            pltpu.VMEM((blocks + 1, CHUNK, 2 * HD), bf16),
+            pltpu.VMEM((tiles, TILE, HD), bf16),
+            pltpu.VMEM((tiles, 2 * HD, TILE), bf16),
+            pltpu.VMEM((tiles, TILE, HD), bf16),
+            pltpu.VMEM((tiles, 2 * HD, TILE), bf16),
+            pltpu.VMEM((2, GROUP, CHUNK, TILE), f32),
+            pltpu.VMEM((2, GROUP, CHUNK, TILE), f32),
+            pltpu.VMEM((blocks + 1, CHUNK, HD), f32),
+            pltpu.VMEM((blocks + 1, CHUNK, HD), f32),
+            pltpu.VMEM((tiles, HD, TILE), f32),
         ],
         compiler_params=params,
         cost_estimate=pl.CostEstimate(
@@ -297,14 +305,16 @@
     first = bounds(tokens)[0] // CHUNK
     last = (bounds(tokens + QBLK - 1)[1] - 1) // CHUNK
     needed = (place[None, :] >= first[:, None]) & (place[None, :] <= last[:, None])
-    needed = (needed[0::2] | needed[1::2]).astype(jnp.int32)
-    count = jnp.sum(needed, axis=1)
-    before = jnp.sum(needed[:, None, :] * (place[None, :] < place[:, None]), axis=2)
-    slots = jnp.arange(blocks + GROUP, dtype=jnp.int32)
-    chosen = (before[:, None, :] == slots[None, :, None]) & (needed[:, None, :] > 0)
-    chunk_list = jnp.sum(jnp.where(chosen, place[None, None, :], 0), axis=2)
-    chunk_list = jnp.where(slots[None, :] < count[:, None], chunk_list, blocks)
-    return order, tokens, count, chunk_list
+    needed = (needed[0::2] | needed[1::2]).astype(jnp.int32).reshape(-1)
+    cells = jnp.arange(needed.shape[0], dtype=jnp.int32)
+    before = jnp.sum(needed[None, :] * (cells[None, :] < cells[:, None]), axis=1)
+    slots = jnp.arange(needed.shape[0] + 2 * GROUP, dtype=jnp.int32)
+    chosen = (before[None, :] == slots[:, None]) & (needed[None, :] > 0)
+    cell = jnp.sum(jnp.where(chosen, cells[None, :], 0), axis=1)
+    total = jnp.sum(needed, keepdims=True)
+    tile = cell // blocks
+    spot = jnp.where(slots < total, cell % blocks, blocks)
+    return order, tokens, (total + GROUP - 1) // GROUP, tile, spot
 
 
 def edges_of(lengths, tokens):

time: 96.1 us -> 94.9 us (0.988)
  Pallas kernels: 34.8 us -> 28.1 us
  starting transfers between devices: 9.06 us -> 11.5 us
  waiting for transfers between devices: 20.4 us -> 22.3 us
  other arithmetic: 3.14 us -> 4.14 us
    pallas_call x1, Pallas kernels: 12.4 us -> 8.25 us  [prepare(): pl.pallas_call(prepare_kernel, out_shape=jax.ShapeDtypeStruct((tiles, 1,...]
    all_to_all x2, waiting for transfers between devices: 14.5 us -> 17.2 us  [exchange(): return lax.all_to_all(x, 'seq', 0, 0, axis_index_groups=groups)]
    pallas_call x1, Pallas kernels: 17.4 us -> 14.9 us  [grads(): pl.pallas_call(grads_kernel, out_shape=(jax.ShapeDtypeStruct((chips, TILE...]
    ppermute x1, starting transfers between devices: 0.09 us -> 2.58 us  [on_device(): received = lax.ppermute(send, 'seq', swap)]
  transfers between devices with their start and end apart: 5 -> 5, of which waited for: 5 -> 5; matrix products, arithmetic and copies ran while one was open for 3% -> 4% of each run, Pallas kernels for 13% -> 9%
where the time goes in v2:
time: 94.9 us; the launch traced here: 94.5 us
  Pallas kernels  28.1 us (30%)
  blocking collectives  25.3 us (27%)
  waiting for transfers between devices  22.3 us (23%)
  starting transfers between devices  11.5 us (12%)
  other arithmetic  4.14 us (4%)
  local copies, waits for them, and re-layouts  1.63 us (2%)
  between operations  1.55 us (2%)
    all_to_all x1, blocking collectives, exchange(): return lax.all_to_all(x, 'seq', 0, 0, axis_index_groups=groups)  25.3 us
    all_to_all x2, waiting for transfers between devices, exchange(): return lax.all_to_all(x, 'seq', 0, 0, axis_index_groups=groups)  17.2 us
    pallas_call x1, Pallas kernels, grads(): pl.pallas_call(grads_kernel, out_shape=(jax.ShapeDtypeStruct((chips, TILE...  14.9 us
    all_to_all x2, starting transfers between devices, exchange(): return lax.all_to_all(x, 'seq', 0, 0, axis_index_groups=groups)  8.8 us
    pallas_call x1, Pallas kernels, prepare(): pl.pallas_call(prepare_kernel, out_shape=jax.ShapeDtypeStruct((tiles, 1,...  8.25 us
    pallas_call x1, Pallas kernels, unpack(): pl.pallas_call(unpack_kernel, out_shape=(jax.ShapeDtypeStruct((rows, head...  2.61 us
    ppermute x1, starting transfers between devices, on_device(): received = lax.ppermute(send, 'seq', swap)  2.58 us
    pallas_call x1, Pallas kernels, pack(): pl.pallas_call(pack_kernel, out_shape=jax.ShapeDtypeStruct((chips, 2 * ro...  2.39 us
  transfers between devices with their start and end apart: 5, of which 5 were waited for; matrix products, arithmetic and copies ran while one was open for 4% of the time, Pallas kernels for 9%

profile of v2, /device:TPU:4, one launch (start us, length us, event | category | flops | bytes accessed | tf_op | source)
XLA Modules:
  0.0 94.5 jit_solution(9175992142810786780)
XLA Ops:
  0.6 2.4 %pack.1 = bf16[8,528,128]{2,1,0:T(8,128)(2,1)} custom-call(s32[2]{0:T(128)} %ids_ref.1, bf16[256,768]{1,0:T(8,128)(2,1)} %k_ref.1, bf16[256,768]{1,0:T(8,128)(2,1)} %q_ref.1), custom_call_target="tpu_custom_call" | custom-call | tf_op jit(solution)/shard_map/pack/pallas_call | solution.py:43
  3.0 5.2 %all-to-all-start = ((bf16[8,528,128]{2,1,0:T(8,128)(2,1)}), bf16[8,528,128]{2,1,0:T(8,128)(2,1)S(1)}, u32[]{:S(2)}, u32[]{:S(2)}) async-start(bf16[8,528,128]{2,1,0:T(8,128)(2,1)} %pack.1), calls=%async_computation | async-start | bytes 2162688 | tf_op jit(solution)/shard_map/all_to_all | solution.py:349
  8.3 0.2 copy.18
  8.5 0.2 copy.21
  8.7 0.2 reduce-window.8
  8.9 0.2 copy.19
  9.2 0.3 copy-done.2
  9.5 0.2 copy.16
  9.6 0.2 copy.17
  10.1 1.1 %fusion.4 = bf16[8,544,128]{2,1,0:T(8,128)(2,1)} fusion(bf16[6,32,128]{2,1,0:T(8,128)(2,1)S(1)} %bitcast.21, bf16[6,256,128]{2,1,0:T(8,128)(2,1)S(1)} %bitcast.19, bf16[6,256,128]{2,1,0:T(8,128)(2,1)S(1)} %bitcast.20), kind=kLoop, calls=%fused_computation.7 | loop fusion | flops 5570560 | bytes 1949696 | tf_op jit(solution)/shard_map/concatenate | solution.py:360
  11.2 13.1 %all-to-all-done.first_ref = bf16[8,528,128]{2,1,0:T(8,128)(2,1)S(1)} async-done(((bf16[8,528,128]{2,1,0:T(8,128)(2,1)}), bf16[8,528,128]{2,1,0:T(8,128)(2,1)S(1)}, u32[]{:S(2)}, u32[]{:S(2)}) %all-to-all-start) | async-done | bytes 1081376 | tf_op jit(solution)/shard_map/all_to_all | solution.py:349
  24.3 0.2 convert_reduce_fusion
  24.6 0.2 convert_reduce_fusion.1
  24.8 0.1 select_reduce_fusion.2
  24.9 0.1 select_reduce_fusion.5
  25.2 3.6 %all-to-all-start.1 = ((bf16[8,544,128]{2,1,0:T(8,128)(2,1)}), bf16[8,544,128]{2,1,0:T(8,128)(2,1)S(1)}, u32[]{:S(2)}, u32[]{:S(2)}) async-start(bf16[8,544,128]{2,1,0:T(8,128)(2,1)} %fusion.4), calls=%async_computation.1 | async-start | bytes 2228224 | tf_op jit(solution)/shard_map/all_to_all | solution.py:349
  28.8 0.6 fusion.14
  30.2 0.1 select_reduce_fusion.1
  30.4 0.1 select_reduce_fusion
  30.5 0.7 compare_select_fusion.2
  31.2 1.0 %collective-permute-done.other_ref = bf16[8,256,128]{2,1,0:T(8,128)(2,1)S(1)} collective-permute-done((bf16[8,256,128]{2,1,0:T(8,128)(2,1)S(1)}, bf16[8,256,128]{2,1,0:T(8,128)(2,1)S(1)}, u32[]{:S(2)}, u32[]{:S(2)}) %collective-permute-start) | collective-permute-done | bytes 524320 | tf_op jit(solution)/shard_map/ppermute | solution.py:368
  32.2 8.3 %prepare.1.level_ref = f32[8,1,256]{2,1,0:T(1,128)S(1)} custom-call(s32[1]{0:T(128)} %bitcast.core_ref, s32[16]{0:T(128)S(1)} %get-tuple-element.20.order_ref, s32[16]{0:T(128)S(1)} %get-tuple-element.27.token_ref, s32[1]{0:T(128)S(6)} %select_n.59.steps_ref, s32[136]{0:T(256)S(1)} %get-tuple-element.25.tile_ref, s32[136]{0:T(256)S(1)} %get-tuple-element.24.spot_ref, ...), custom_call_target="tpu_custom_call" | custom-call | flops 2147483648 | bytes 8388608 | tf_op jit(solution)/shard_map/prepare/pallas_call | solution.py:149
  40.5 4.0 %all-to-all-done.1.second_ref = bf16[8,544,128]{2,1,0:T(8,128)(2,1)S(1)} async-done(((bf16[8,544,128]{2,1,0:T(8,128)(2,1)}), bf16[8,544,128]{2,1,0:T(8,128)(2,1)S(1)}, u32[]{:S(2)}, u32[]{:S(2)}) %all-to-all-start.1) | async-done | bytes 1114144 | tf_op jit(solution)/shard_map/all_to_all | solution.py:349
  44.5 0.1 collective-permute-start.1
  44.6 1.9 %collective-permute-done.1.second_other = bf16[8,256,128]{2,1,0:T(8,128)(2,1)S(1)} collective-permute-done((bf16[8,256,128]{2,1,0:T(8,128)(2,1)S(1)}, bf16[8,256,128]{2,1,0:T(8,128)(2,1)S(1)}, u32[]{:S(2)}, u32[]{:S(2)}) %collective-permute-start.1) | collective-permute-done | bytes 524320 | tf_op jit(solution)/shard_map/ppermute | solution.py:371
  46.5 14.9 %grads.1 = (bf16[8,256,128]{2,1,0:T(8,128)(2,1)S(1)}, f32[8,512,128]{2,1,0:T(8,128)S(1)}, bf16[8,512,128]{2,1,0:T(8,128)(2,1)S(1)}) custom-call(s32[1]{0:T(128)} %bitcast.core_ref, s32[16]{0:T(128)S(1)} %get-tuple-element.20.order_ref, s32[16]{0:T(128)S(1)} %get-tuple-element.27.token_ref, s32[1]{0:T(128)S(6)} %select_n.59.steps_ref, ...), custom_call_target="tpu_custom_call" | custom-call | flops 5368709120 | bytes 10485760 | tf_op jit(solution)/shard_map/grads/pallas_call | solution.py:260
  61.4 2.6 %collective-permute-start.2 = (bf16[8,512,128]{2,1,0:T(8,128)(2,1)S(1)}, bf16[8,512,128]{2,1,0:T(8,128)(2,1)S(1)}, u32[]{:S(2)}, u32[]{:S(2)}) collective-permute-start(bf16[8,512,128]{2,1,0:T(8,128)(2,1)S(1)} %get-tuple-element.16), channel_id=1, source_target_pairs={{0,4},{4,0},{8,12},{12,8},{16,20},{20,16},{24,28},{28,24},{32,36},... | collective-permute-start | bytes 3145736 | tf_op jit(solution)/shard_map/ppermute | solution.py:376
  64.0 2.3 %collective-permute-done.2 = bf16[8,512,128]{2,1,0:T(8,128)(2,1)S(1)} collective-permute-done((bf16[8,512,128]{2,1,0:T(8,128)(2,1)S(1)}, bf16[8,512,128]{2,1,0:T(8,128)(2,1)S(1)}, u32[]{:S(2)}, u32[]{:S(2)}) %collective-permute-start.2) | collective-permute-done | bytes 1048608 | tf_op jit(solution)/shard_map/ppermute | solution.py:376
  66.3 0.3 add_convert_fusion
  66.5 0.1 pad_maximum_fusion
  66.6 25.3 %all_to_all.15.x_ref = bf16[8,768,128]{2,1,0:T(8,128)(2,1)} all-to-all(bf16[8,768,128]{2,1,0:T(8,128)(2,1)S(1)} %pad_maximum_fusion), channel_id=1, replica_groups={{0,8,16,24,32,40,48,56},{4,12,20,28,36,44,52,60},{1,9,17,25,33,41,49,57..., dimensions={0} | all-to-all | bytes 3145728 | tf_op jit(solution)/shard_map/all_to_all | solution.py:349
  91.9 2.6 %unpack.1 = (bf16[256,768]{1,0:T(8,128)(2,1)}, bf16[256,768]{1,0:T(8,128)(2,1)}, bf16[256,768]{1,0:T(8,128)(2,1)}) custom-call(bf16[8,768,128]{2,1,0:T(8,128)(2,1)} %all_to_all.15.x_ref), custom_call_target="tpu_custom_call" | custom-call | tf_op jit(solution)/shard_map/unpack/pallas_call | solution.py:62
  (29 shorter events, 0.8 us)
Async XLA Ops:
  0.6 7.6 %copy-start = (bf16[256,768]{1,0:T(8,128)(2,1)S(1)}, bf16[256,768]{1,0:T(8,128)(2,1)}, u32[]{:S(2)}) copy-start(bf16[256,768]{1,0:T(8,128)(2,1)} %param.11) | copy-start | bytes 1179652
  3.0 5.4 %copy-start.1 = (bf16[256,768]{1,0:T(8,128)(2,1)S(1)}, bf16[256,768]{1,0:T(8,128)(2,1)}, u32[]{:S(2)}) copy-start(bf16[256,768]{1,0:T(8,128)(2,1)} %param.10) | copy-start | bytes 1179652
  3.0 5.6 %copy-start.3 = (s32[8]{0:T(128)S(1)}, s32[8]{0:T(128)}, u32[]{:S(2)}) copy-start(s32[8]{0:T(128)} %param.12) | copy-start | bytes 100
  3.0 21.3 %all-to-all-start = ((bf16[8,528,128]{2,1,0:T(8,128)(2,1)}), bf16[8,528,128]{2,1,0:T(8,128)(2,1)S(1)}, u32[]{:S(2)}, u32[]{:S(2)}) async-start(bf16[8,528,128]{2,1,0:T(8,128)(2,1)} %pack.1), calls=%async_computation | async-start | bytes 2162688 | tf_op jit(solution)/shard_map/all_to_all | solution.py:349
  8.5 1.0 %copy-start.2 = (bf16[256,768]{1,0:T(8,128)(2,1)S(1)}, bf16[256,768]{1,0:T(8,128)(2,1)}, u32[]{:S(2)}) copy-start(bf16[256,768]{1,0:T(8,128)(2,1)} %param.9) | copy-start | bytes 1179652
  25.2 19.3 %all-to-all-start.1 = ((bf16[8,544,128]{2,1,0:T(8,128)(2,1)}), bf16[8,544,128]{2,1,0:T(8,128)(2,1)S(1)}, u32[]{:S(2)}, u32[]{:S(2)}) async-start(bf16[8,544,128]{2,1,0:T(8,128)(2,1)} %fusion.4), calls=%async_computation.1 | async-start | bytes 2228224 | tf_op jit(solution)/shard_map/all_to_all | solution.py:349
  30.2 1.9 %collective-permute-start = (bf16[8,256,128]{2,1,0:T(8,128)(2,1)S(1)}, bf16[8,256,128]{2,1,0:T(8,128)(2,1)S(1)}, u32[]{:S(2)}, u32[]{:S(2)}) collective-permute-start(bf16[8,256,128]{2,1,0:T(8,128)(2,1)S(1)} %slice.18), channel_id=1, source_target_pairs={{0,4},{4,0},{8,12},{12,8},{16,20},{20,16},{24,28},{28,24},{32,36},... | collective-permute-start | bytes 1572872 | tf_op jit(solution)/shard_map/ppermute | solution.py:368
  44.5 2.0 %collective-permute-start.1 = (bf16[8,256,128]{2,1,0:T(8,128)(2,1)S(1)}, bf16[8,256,128]{2,1,0:T(8,128)(2,1)S(1)}, u32[]{:S(2)}, u32[]{:S(2)}) collective-permute-start(bf16[8,256,128]{2,1,0:T(8,128)(2,1)S(1)} %slice.19), channel_id=1, source_target_pairs={{0,4},{4,0},{8,12},{12,8},{16,20},{20,16},{24,28},{28,24},{32,36},... | collective-permute-start | bytes 1572872 | tf_op jit(solution)/shard_map/ppermute | solution.py:371
  61.4 4.9 %collective-permute-start.2 = (bf16[8,512,128]{2,1,0:T(8,128)(2,1)S(1)}, bf16[8,512,128]{2,1,0:T(8,128)(2,1)S(1)}, u32[]{:S(2)}, u32[]{:S(2)}) collective-permute-start(bf16[8,512,128]{2,1,0:T(8,128)(2,1)S(1)} %get-tuple-element.16), channel_id=1, source_target_pairs={{0,4},{4,0},{8,12},{12,8},{16,20},{20,16},{24,28},{28,24},{32,36},... | collective-permute-start | bytes 3145736 | tf_op jit(solution)/shard_map/ppermute | solution.py:376

commit v3 on v2

v3 whole, which is shorter than its diff:
```python
import math

import jax
import jax.numpy as jnp
from jax import lax
from jax.experimental import pallas as pl
from jax.experimental.pallas import tpu as pltpu
from jax.sharding import PartitionSpec as P

HD = 128
QBLK = 128
CHUNK = 256
TILE = 2 * QBLK
GROUP = 4
WIDE = 6
SCALE = HD ** (-0.5)
RATE = SCALE * math.log2(math.e)
FLOOR = -1e30
EXTRA = 16

smem = pl.BlockSpec(memory_space=pltpu.SMEM)
vmem = pl.BlockSpec(memory_space=pltpu.VMEM)
params = pltpu.CompilerParams(vmem_limit_bytes=32 * 1024 * 1024)
small = pltpu.CompilerParams(vmem_limit_bytes=4 * 1024 * 1024)


def dot(a, b):
    return jnp.dot(a, b, preferred_element_type=jnp.float32)


def pack_kernel(ids_ref, k_ref, q_ref, out_ref):
    rows = k_ref.shape[0]
    heads = k_ref.shape[1] // HD
    line = lax.broadcasted_iota(jnp.int32, (EXTRA, HD), 0)
    note = jnp.where(line == 0, ids_ref[0], ids_ref[1]).astype(jnp.float32).astype(out_ref.dtype)
    for slot in range(out_ref.shape[0]):
        columns = slice(slot % heads * HD, (slot % heads + 1) * HD)
        out_ref[slot, :rows, :] = k_ref[:, columns]
        out_ref[slot, rows : 2 * rows, :] = q_ref[:, columns]
        out_ref[slot, 2 * rows :, :] = note


def pack(ids, k, q, chips):
    rows = k.shape[0]
    return pl.pallas_call(
        pack_kernel,
        out_shape=jax.ShapeDtypeStruct((chips, 2 * rows + EXTRA, HD), k.dtype),
        in_specs=[smem, vmem, vmem],
        out_specs=vmem,
        name="pack",
    )(ids, k, q)


def unpack_kernel(x_ref, *out_refs):
    rows, width = out_refs[0].shape
    for i, out_ref in enumerate(out_refs):
        for head in range(width // HD):
            columns = slice(head * HD, (head + 1) * HD)
            out_ref[:, columns] = x_ref[head, i * rows : (i + 1) * rows, :]


def unpack(x, rows, heads):
    number = x.shape[1] // rows
    return pl.pallas_call(
        unpack_kernel,
        out_shape=(jax.ShapeDtypeStruct((rows, heads * HD), x.dtype),) * number,
        in_specs=[vmem],
        out_specs=(vmem,) * number,
        compiler_params=small,
        name="unpack",
    )(x)


def place_key(keys, slot, spot, k, edges):
    rows = lax.broadcasted_iota(jnp.int32, (CHUNK, HD), 0) + spot * CHUNK
    outside = (rows < edges[0:1]) | (rows >= edges[1:2])
    keys[slot, :, :HD] = k
    keys[slot, :, HD:] = jnp.where(outside, 1.0, 0.0).astype(jnp.bfloat16)


def place_query(qt, slot, q, token, sides):
    rows = slice(slot * QBLK, (slot + 1) * QBLK)
    tokens = lax.broadcasted_iota(jnp.int32, (EXTRA, QBLK), 1) + token
    within = (tokens >= sides[:EXTRA]) & (tokens < sides[EXTRA:])
    qt[:HD, rows] = q.T
    qt[HD : HD + EXTRA, rows] = jnp.where(within, FLOOR, 0.0).astype(jnp.bfloat16)


def block_rows(block, base, size):
    return pl.ds(pl.multiple_of(base + block % 2 * size, size), size)


def fetch(own, other, block, base, size):
    blocks = 2 * own.shape[0]
    here = block % blocks
    mine = own[here // 2, block_rows(here, CHUNK + base, size), :]
    theirs = other[here // 2, block_rows(here, base, size), :]
    return jnp.where(block < blocks, mine, theirs)


def prepare_kernel(
    core_ref, order_ref, units_ref, tile_ref, spot_ref, first_ref, other_ref, edges, sides,
    stats_ref,
    keys, qt, raw, tops, totals,
):
    core = core_ref[0]
    chips = first_ref.shape[0]
    tiles = stats_ref.shape[0]

    def place(i, carry):
        place_key(keys, i, 2 * i + core, first_ref[i, :CHUNK, :], edges)
        for t in (2 * i, 2 * i + 1):
            for slot in range(2):
                q = fetch(first_ref, other_ref, order_ref[2 * t + slot], 0, QBLK)
                place_query(qt.at[t], slot, q, (2 * t + slot) * QBLK, sides)
            qt[t, HD + EXTRA :, :] = jnp.zeros((HD - EXTRA, TILE), jnp.bfloat16)
            tops[t] = jnp.full((8, TILE), FLOOR, jnp.float32)
            totals[t] = jnp.zeros((8, TILE), jnp.float32)
        return carry

    lax.fori_loop(0, chips, place, 0)
    keys[chips] = jnp.ones((CHUNK, 2 * HD), jnp.bfloat16)

    def score(i, u):
        return dot(keys[spot_ref[GROUP * i + u]], qt[tile_ref[GROUP * i + u]])

    for u in range(GROUP):
        raw[0, u] = score(0, u)

    def step(i, carry):
        parts = []
        for u in range(GROUP):
            s = raw[i % 2, u].reshape(4, 8, 8, TILE)
            top = jnp.max(jnp.max(s, axis=1), axis=0)
            total = jnp.sum(jnp.sum(jnp.exp2((s - top) * RATE), axis=1), axis=0)
            parts.append((top, total))
        for u in range(GROUP):
            raw[(i + 1) % 2, u] = score(i + 1, u)
        for u, (top, total) in enumerate(parts):
            t = tile_ref[GROUP * i + u]
            old = tops[t]
            new = jnp.maximum(old, top)
            totals[t] = totals[t] * jnp.exp2((old - new) * RATE) + total * jnp.exp2((top - new) * RATE)
            tops[t] = new
        return carry

    lax.fori_loop(0, (units_ref[0] + GROUP - 1) // GROUP, step, 0)
    for t in range(tiles):
        top = tops[t]
        row_top = jnp.max(top, axis=0, keepdims=True)
        stats_ref[t, 0:1] = row_top
        stats_ref[t, 1:2] = jnp.sum(
            totals[t] * jnp.exp2((top - row_top) * RATE), axis=0, keepdims=True
        )


def prepare(scalars, first, other, edges, sides):
    chips = first.shape[0]
    tiles = 2 * chips
    pairs = tiles * TILE * 1024
    return pl.pallas_call(
        prepare_kernel,
        out_shape=jax.ShapeDtypeStruct((tiles, 2, TILE), jnp.float32),
        in_specs=[smem] * len(scalars) + [vmem] * 4,
        out_specs=vmem,
        scratch_shapes=[
            pltpu.VMEM((chips + 1, CHUNK, 2 * HD), jnp.bfloat16),
            pltpu.VMEM((tiles, 2 * HD, TILE), jnp.bfloat16),
            pltpu.VMEM((2, GROUP, CHUNK, TILE), jnp.float32),
            pltpu.VMEM((tiles, 8, TILE), jnp.float32),
            pltpu.VMEM((tiles, 8, TILE), jnp.float32),
        ],
        compiler_params=params,
        cost_estimate=pl.CostEstimate(
            flops=4 * pairs * HD, bytes_accessed=8 * 2**20, transcendentals=pairs
        ),
        name="prepare",
    )(*scalars, first, other, edges, sides)


def grads_kernel(
    core_ref, order_ref, units_ref, tile_ref, spot_ref, first_ref, other_ref, edges, sides,
    second_ref, second_other, stats_ref, stats_other,
    keep_ref, send_ref, dkv_ref,
    keys, keys_t, values, qs, qt, gs, gt, level, raw, slope, acc_k, acc_v, acc_q,
):
    core = core_ref[0]
    chips = first_ref.shape[0]

    def place(i, carry):
        k = first_ref[i, :CHUNK, :]
        place_key(keys, i, 2 * i + core, k, edges)
        keys_t[i] = k.T
        values[i, :, :HD] = second_ref[i, :CHUNK, :]
        values[i, :, HD:] = jnp.full((CHUNK, HD), -1, jnp.bfloat16)
        acc_k[i] = jnp.zeros((CHUNK, HD), jnp.float32)
        acc_v[i] = jnp.zeros((CHUNK, HD), jnp.float32)
        for t in (2 * i, 2 * i + 1):
            acc_q[t] = jnp.zeros((HD, TILE), jnp.float32)
            for slot in range(2):
                block = order_ref[2 * t + slot]
                rows = slice(slot * QBLK, (slot + 1) * QBLK)
                q = fetch(first_ref, other_ref, block, 0, QBLK)
                g = fetch(second_ref, second_other, block, 0, QBLK)
                qs[t, rows, :] = q
                gs[t, rows, :] = g
                place_query(qt.at[t], slot, q, (2 * t + slot) * QBLK, sides)
                gt[t, :HD, rows] = g.T
                gt[t, HD : HD + EXTRA, rows] = fetch(second_ref, second_other, block, CHUNK, EXTRA)
            for ref in (qt, gt):
                ref[t, HD + EXTRA :, :] = jnp.zeros((HD - EXTRA, TILE), jnp.bfloat16)
            tops = [ref[t, 0:1] for ref in (stats_ref, stats_other)]
            top = jnp.maximum(*tops)
            total = sum(
                ref[t, 1:2] * jnp.exp2((x - top) * RATE)
                for x, ref in zip(tops, (stats_ref, stats_other))
            )
            level[t] = top + jnp.log2(total) * (1.0 / RATE)
        return carry

    lax.fori_loop(0, chips, place, 0)
    keys[chips] = jnp.ones((CHUNK, 2 * HD), jnp.bfloat16)
    keys_t[chips] = jnp.zeros((HD, CHUNK), jnp.bfloat16)
    values[chips] = jnp.zeros((CHUNK, 2 * HD), jnp.bfloat16)
    acc_k[chips] = jnp.zeros((CHUNK, HD), jnp.float32)
    acc_v[chips] = jnp.zeros((CHUNK, HD), jnp.float32)

    def unit(i, u):
        return tile_ref[WIDE * i + u], spot_ref[WIDE * i + u]

    def ahead(i):
        for u in range(WIDE):
            t, spot = unit(i, u)
            raw[i % 2, u] = dot(keys[spot], qt[t])
            slope[i % 2, u] = dot(values[spot], gt[t])

    ahead(0)

    def work(i):
        for u in range(WIDE):
            t, spot = unit(i, u)
            p = jnp.exp2((raw[i % 2, u] - level[t]) * RATE)
            s = (p * slope[i % 2, u]).astype(jnp.bfloat16)
            acc_v[spot] += dot(p.astype(jnp.bfloat16), gs[t])
            acc_k[spot] += dot(s, qs[t])
            acc_q[t] += dot(keys_t[spot], s)

    def step(i, carry):
        work(i)
        ahead(i + 1)
        return carry

    last = (units_ref[0] + WIDE - 1) // WIDE - 1
    lax.fori_loop(0, last, step, 0)
    work(last)

    def hand_out(i, carry):
        dkv_ref[i, :CHUNK] = (acc_k[i] * SCALE).astype(jnp.bfloat16)
        dkv_ref[i, CHUNK:] = acc_v[i].astype(jnp.bfloat16)
        for t in (2 * i, 2 * i + 1):
            result = (acc_q[t] * SCALE).T
            for slot in range(2):
                block = order_ref[2 * t + slot]
                here = block % (2 * chips)
                rows = block_rows(here, 0, QBLK)
                part = result[slot * QBLK : (slot + 1) * QBLK]
                mine = block < 2 * chips
                keep_ref[jnp.where(mine, here // 2, chips), rows, :] = part
                send_ref[jnp.where(mine, chips, here // 2), rows, :] = part.astype(jnp.bfloat16)
        return carry

    lax.fori_loop(0, chips, hand_out, 0)


def grads(scalars, first, other, edges, sides, second, second_other, stats, stats_other):
    chips = second.shape[0]
    tiles = 2 * chips
    pairs = tiles * TILE * 1024
    bf16, f32 = jnp.bfloat16, jnp.float32
    return pl.pallas_call(
        grads_kernel,
        out_shape=(
            jax.ShapeDtypeStruct((chips + 1, TILE, HD), f32),
            jax.ShapeDtypeStruct((chips + 1, TILE, HD), bf16),
            jax.ShapeDtypeStruct((chips, 2 * CHUNK, HD), bf16),
        ),
        in_specs=[smem] * len(scalars) + [vmem] * 8,
        out_specs=(vmem,) * 3,
        scratch_shapes=[
            pltpu.VMEM((chips + 1, CHUNK, 2 * HD), bf16),
            pltpu.VMEM((chips + 1, HD, CHUNK), bf16),
            pltpu.VMEM((chips + 1, CHUNK, 2 * HD), bf16),
            pltpu.VMEM((tiles, TILE, HD), bf16),
            pltpu.VMEM((tiles, 2 * HD, TILE), bf16),
            pltpu.VMEM((tiles, TILE, HD), bf16),
            pltpu.VMEM((tiles, 2 * HD, TILE), bf16),
            pltpu.VMEM((tiles, 1, TILE), f32),
            pltpu.VMEM((2, WIDE, CHUNK, TILE), f32),
            pltpu.VMEM((2, WIDE, CHUNK, TILE), f32),
            pltpu.VMEM((chips + 1, CHUNK, HD), f32),
            pltpu.VMEM((chips + 1, CHUNK, HD), f32),
            pltpu.VMEM((tiles, HD, TILE), f32),
        ],
        compiler_params=params,
        cost_estimate=pl.CostEstimate(
            flops=10 * pairs * HD, bytes_accessed=10 * 2**20, transcendentals=pairs
        ),
        name="grads",
    )(*scalars, first, other, edges, sides, second, second_other, stats, stats_other)


def plan(lengths, core, chips):
    ends = jnp.cumsum(lengths)
    offsets = ends - lengths
    place = jnp.arange(2 * chips, dtype=jnp.int32)

    def bounds(token):
        inside = (token[:, None] >= offsets) & (token[:, None] < ends)
        return [jnp.sum(jnp.where(inside, x, 0), axis=1) for x in (offsets, ends)]

    first = bounds(place * TILE)[0] // CHUNK
    last = (bounds(place * TILE + TILE - 1)[1] - 1) // CHUNK
    chunks = 2 * jnp.arange(chips, dtype=jnp.int32) + core
    needed = (chunks[None, :] >= first[:, None]) & (chunks[None, :] <= last[:, None])
    needed = needed.astype(jnp.int32).reshape(-1)
    cells = jnp.arange(needed.shape[0], dtype=jnp.int32)
    before = jnp.sum(needed[None, :] * (cells[None, :] < cells[:, None]), axis=1)
    slots = jnp.arange(needed.shape[0] + 2 * max(GROUP, WIDE), dtype=jnp.int32)
    chosen = (before[None, :] == slots[:, None]) & (needed[None, :] > 0)
    cell = jnp.sum(jnp.where(chosen, cells[None, :], 0), axis=1)
    total = jnp.sum(needed, keepdims=True)
    spot = jnp.where(slots < total, cell % chips, chips)
    return total, cell // chips, spot


def edges_of(lengths, tokens):
    ends = jnp.cumsum(lengths)
    offsets = ends - lengths
    spare = HD - lengths.shape[0]
    edges = jnp.stack([jnp.pad(offsets, (0, spare)), jnp.pad(ends, (0, spare), constant_values=tokens)])
    spare = EXTRA - lengths.shape[0]
    sides = [jnp.pad(x, (0, spare), constant_values=tokens) for x in (offsets, ends)]
    return edges, jnp.broadcast_to(jnp.concatenate(sides)[:, None], (2 * EXTRA, QBLK))


def split_in_three(x):
    parts = []
    for _ in range(3):
        part = lax.reduce_precision(x, exponent_bits=8, mantissa_bits=7)
        parts.append(part.astype(jnp.bfloat16))
        x = x - part
    return jnp.stack(parts, axis=-2)


def on_device(queries, keys_in, values_in, forward_out, grad_out, lengths, query_block):
    size = lax.axis_size("seq")
    chips = size // 2
    core = lax.axis_index("seq") % 2
    rows = queries.shape[0]
    heads = queries.shape[1] // HD
    groups = [[2 * i + c for i in range(chips)] for c in range(2)]
    swap = [(i, i ^ 1) for i in range(size)]

    def exchange(x):
        return lax.all_to_all(x, "seq", 0, 0, axis_index_groups=groups)

    first = exchange(pack(query_block, keys_in, queries, chips))

    delta = jnp.sum(
        (grad_out.astype(jnp.float32) * forward_out.astype(jnp.float32)).reshape(rows, heads, HD),
        axis=2,
    )
    parts = split_in_three(delta.T.reshape(heads, rows // QBLK, QBLK))
    parts = jnp.pad(parts, ((0, 0), (0, 0), (0, EXTRA - 3), (0, 0))).reshape(heads, -1, HD)
    by_head = [x.reshape(rows, heads, HD).transpose(1, 0, 2) for x in (values_in, grad_out)]
    second = jnp.concatenate(by_head + [parts], axis=1)
    second = jnp.pad(second, ((0, chips - heads), (0, 0), (0, 0)))
    first, second = lax.optimization_barrier((first, second))
    second = exchange(second)

    other = lax.ppermute(first[:, rows:], "seq", swap)
    ids = jnp.concatenate([first[:, 2 * rows : 2 * rows + 2, 0], other[:, rows : rows + 2, 0]])
    ids = ids.astype(jnp.int32).reshape(-1)
    place = jnp.arange(ids.shape[0], dtype=jnp.int32)
    order = jnp.sum(jnp.where(ids[None, :] == place[:, None], place[None, :], 0), axis=1)
    units, tile, spot = plan(lengths, core, chips)
    scalars = (jnp.full((1,), core, jnp.int32), order, units, tile, spot)
    edges, sides = edges_of(lengths, size * rows)
    stats = prepare(scalars, first, other, edges, sides)
    stats_other = lax.ppermute(stats, "seq", swap)
    second, stats = lax.optimization_barrier((second, stats))
    second_other = lax.ppermute(second[:, rows:], "seq", swap)
    keep, send, dkv = grads(
        scalars, first, other, edges, sides, second, second_other, stats, stats_other
    )

    received = lax.ppermute(send, "seq", swap)
    dq = (keep + received.astype(jnp.float32))[:chips].astype(jnp.bfloat16)
    return unpack(exchange(jnp.concatenate([dq, dkv], axis=1)), rows, heads)


def solution(mesh):
    spec = P(("win", "seq"), "head")
    in_specs = (spec,) * 5 + (P("win"), P(("win", "seq")))
    return jax.shard_map(
        on_device, mesh=mesh, in_specs=in_specs, out_specs=(spec,) * 3, check_vma=False
    )
```

time: 94.9 us -> 89.7 us (0.945)
  waiting for transfers between devices: 22.3 us -> 20.1 us
  starting transfers between devices: 11.5 us -> 9.55 us
  blocking collectives: 25.3 us -> 24.3 us
    ppermute x1, starting transfers between devices: 2.58 us -> 0.09 us  [on_device(): received = lax.ppermute(send, 'seq', swap)]
    pallas_call x2, Pallas kernels: 23.1 us -> 25.3 us  [the longest x1 15.5 us: grads(): pl.pallas_call(grads_kernel, out_shape=(jax.ShapeDtypeStruct((chips + 1,...]
    pallas_call x1, Pallas kernels: 2.61 us -> 1.21 us  [unpack(): pl.pallas_call(unpack_kernel, out_shape=(jax.ShapeDtypeStruct((rows, head...]
    ppermute x2 -> x3, waiting for transfers between devices: 2.87 us -> 1.81 us  [the longest x1 1.54 us: on_device(): stats_other = lax.ppermute(stats, 'seq', swap)]
  transfers between devices with their start and end apart: 5 -> 6, of which waited for: 5 -> 5; matrix products, arithmetic and copies ran while one was open for 4% -> 6% of each run, Pallas kernels for 9% -> 11%
where the time goes in v3:
time: 89.7 us; the launch traced here: 89.1 us
  Pallas kernels  28.8 us (32%)
  blocking collectives  24.3 us (27%)
  waiting for transfers between devices  20.1 us (22%)
  starting transfers between devices  9.55 us (11%)
  other arithmetic  3.73 us (4%)
  local copies, waits for them, and re-layouts  1.78 us (2%)
    all_to_all x1, blocking collectives, exchange(): return lax.all_to_all(x, 'seq', 0, 0, axis_index_groups=groups)  24.3 us
    all_to_all x2, waiting for transfers between devices, exchange(): return lax.all_to_all(x, 'seq', 0, 0, axis_index_groups=groups)  16.3 us
    pallas_call x1, Pallas kernels, grads(): pl.pallas_call(grads_kernel, out_shape=(jax.ShapeDtypeStruct((chips + 1,...  15.5 us
    pallas_call x1, Pallas kernels, prepare(): pl.pallas_call(prepare_kernel, out_shape=jax.ShapeDtypeStruct((tiles, 2,...  9.75 us
    all_to_all x2, starting transfers between devices, exchange(): return lax.all_to_all(x, 'seq', 0, 0, axis_index_groups=groups)  8.8 us
    pallas_call x1, Pallas kernels, pack(): pl.pallas_call(pack_kernel, out_shape=jax.ShapeDtypeStruct((chips, 2 * ro...  2.34 us
    ppermute x1, waiting for transfers between devices, on_device(): received = lax.ppermute(send, 'seq', swap)  1.99 us
  transfers between devices with their start and end apart: 6, of which 5 were waited for; matrix products, arithmetic and copies ran while one was open for 6% of the time, Pallas kernels for 11%

profile of v3, /device:TPU:4, one launch (start us, length us, event | category | flops | bytes accessed | tf_op | source)
XLA Modules:
  0.0 89.1 jit_solution(18131152404024483107)
XLA Ops:
  0.6 2.3 %pack.1 = bf16[8,528,128]{2,1,0:T(8,128)(2,1)} custom-call(s32[2]{0:T(128)} %ids_ref.1, bf16[256,768]{1,0:T(8,128)(2,1)} %k_ref.1, bf16[256,768]{1,0:T(8,128)(2,1)} %q_ref.1), custom_call_target="tpu_custom_call" | custom-call | tf_op jit(solution)/shard_map/pack/pallas_call | solution.py:45
  3.0 5.2 %all-to-all-start = ((bf16[8,528,128]{2,1,0:T(8,128)(2,1)}), bf16[8,528,128]{2,1,0:T(8,128)(2,1)S(1)}, u32[]{:S(2)}, u32[]{:S(2)}) async-start(bf16[8,528,128]{2,1,0:T(8,128)(2,1)} %pack.1), calls=%async_computation | async-start | bytes 2162688 | tf_op jit(solution)/shard_map/all_to_all | solution.py:365
  8.3 0.2 reduce-window.8
  8.6 0.1 reshape.215
  8.7 0.2 copy.24
  8.9 0.2 copy.25
  9.2 0.2 copy.22
  9.3 0.2 copy.23
  9.6 0.2 copy-done.2
  9.7 0.2 copy.27
  10.2 0.1 select_reduce_fusion.1
  10.3 1.1 %fusion.4 = bf16[8,544,128]{2,1,0:T(8,128)(2,1)} fusion(bf16[6,32,128]{2,1,0:T(8,128)(2,1)S(1)} %bitcast.23, bf16[6,256,128]{2,1,0:T(8,128)(2,1)S(1)} %bitcast.21, bf16[6,256,128]{2,1,0:T(8,128)(2,1)S(1)} %bitcast.22), kind=kLoop, calls=%fused_computation.6 | loop fusion | flops 5570560 | bytes 1949696 | tf_op jit(solution)/shard_map/concatenate | solution.py:376
  11.4 12.9 %all-to-all-done.first_ref = bf16[8,528,128]{2,1,0:T(8,128)(2,1)S(1)} async-done(((bf16[8,528,128]{2,1,0:T(8,128)(2,1)}), bf16[8,528,128]{2,1,0:T(8,128)(2,1)S(1)}, u32[]{:S(2)}, u32[]{:S(2)}) %all-to-all-start) | async-done | bytes 1081376 | tf_op jit(solution)/shard_map/all_to_all | solution.py:365
  24.3 3.6 %all-to-all-start.1 = ((bf16[8,544,128]{2,1,0:T(8,128)(2,1)}), bf16[8,544,128]{2,1,0:T(8,128)(2,1)S(1)}, u32[]{:S(2)}, u32[]{:S(2)}) async-start(bf16[8,544,128]{2,1,0:T(8,128)(2,1)} %fusion.4), calls=%async_computation.1 | async-start | bytes 2228224 | tf_op jit(solution)/shard_map/all_to_all | solution.py:365
  28.1 0.1 select_reduce_fusion
  28.2 0.7 fusion.14
  28.9 0.7 compare_select_fusion.2
  29.6 0.1 copy.28
  29.7 0.3 collective-permute-done.other_ref
  29.9 0.1 copy.29
  30.2 0.1 reshape.214
  30.3 0.1 select_reduce_fusion.2.order_ref
  30.5 9.7 %prepare.1.stats_ref = f32[16,2,256]{2,1,0:T(2,128)S(1)} custom-call(s32[1]{0:T(128)} %bitcast.core_ref, s32[32]{0:T(128)S(1)} %select_reduce_fusion.2.order_ref, s32[1]{0:T(128)} %bitcast.12.units_ref, s32[140]{0:T(256)S(1)} %get-tuple-element.23.tile_ref, s32[140]{0:T(256)S(1)} %get-tuple-element.22.spot_ref, ...), custom_call_target="tpu_custom_call" | custom-call | flops 2147483648 | bytes 8388608 | tf_op jit(solution)/shard_map/prepare/pallas_call | solution.py:161
  40.2 3.4 %all-to-all-done.1.second_ref = bf16[8,544,128]{2,1,0:T(8,128)(2,1)S(1)} async-done(((bf16[8,544,128]{2,1,0:T(8,128)(2,1)}), bf16[8,544,128]{2,1,0:T(8,128)(2,1)S(1)}, u32[]{:S(2)}, u32[]{:S(2)}) %all-to-all-start.1) | async-done | bytes 1114144 | tf_op jit(solution)/shard_map/all_to_all | solution.py:365
  43.7 0.5 collective-permute-start.2
  44.2 1.5 %collective-permute-done.2.stats_other = f32[16,2,256]{2,1,0:T(2,128)S(1)} collective-permute-done((f32[16,2,256]{2,1,0:T(2,128)S(1)}, f32[16,2,256]{2,1,0:T(2,128)S(1)}, u32[]{:S(2)}, u32[]{:S(2)}) %collective-permute-start.2) | collective-permute-done | bytes 32800 | tf_op jit(solution)/shard_map/ppermute | solution.py:390
  45.8 15.5 %grads.1 = (f32[9,256,128]{2,1,0:T(8,128)S(1)}, bf16[9,256,128]{2,1,0:T(8,128)(2,1)S(1)}, bf16[8,512,128]{2,1,0:T(8,128)(2,1)S(1)}) custom-call(s32[1]{0:T(128)} %bitcast.core_ref, s32[32]{0:T(128)S(1)} %select_reduce_fusion.2.order_ref, s32[1]{0:T(128)} %bitcast.12.units_ref, s32[140]{0:T(256)S(1)} %get-tuple-element.23.tile_ref, ...), custom_call_target="tpu_custom_call" | custom-call | flops 5368709120 | bytes 10485760 | tf_op jit(solution)/shard_map/grads/pallas_call | solution.py:280
  61.4 2.0 %collective-permute-done.3 = bf16[9,256,128]{2,1,0:T(8,128)(2,1)S(1)} collective-permute-done((bf16[9,256,128]{2,1,0:T(8,128)(2,1)S(1)}, bf16[9,256,128]{2,1,0:T(8,128)(2,1)S(1)}, u32[]{:S(2)}, u32[]{:S(2)}) %collective-permute-start.3) | collective-permute-done | bytes 589856 | tf_op jit(solution)/shard_map/ppermute | solution.py:397
  63.4 0.1 fusion.5
  63.5 0.1 pad_maximum_fusion
  63.6 24.3 %all_to_all.15.x_ref = bf16[8,768,128]{2,1,0:T(8,128)(2,1)S(1)} all-to-all(bf16[8,768,128]{2,1,0:T(8,128)(2,1)S(1)} %pad_maximum_fusion), channel_id=1, replica_groups={{0,8,16,24,32,40,48,56},{4,12,20,28,36,44,52,60},{1,9,17,25,33,41,49,57..., dimensions={0} | all-to-all | bytes 3145728 | tf_op jit(solution)/shard_map/all_to_all | solution.py:365
  87.9 1.2 %unpack.1 = (bf16[256,768]{1,0:T(8,128)(2,1)}, bf16[256,768]{1,0:T(8,128)(2,1)}, bf16[256,768]{1,0:T(8,128)(2,1)}) custom-call(bf16[8,768,128]{2,1,0:T(8,128)(2,1)S(1)} %all_to_all.15.x_ref), custom_call_target="tpu_custom_call" | custom-call | tf_op jit(solution)/shard_map/unpack/pallas_call | solution.py:64
  (34 shorter events, 1.1 us)
Async XLA Ops:
  0.6 7.6 %copy-start.3 = (s32[8]{0:T(128)S(1)}, s32[8]{0:T(128)}, u32[]{:S(2)}) copy-start(s32[8]{0:T(128)} %param.12) | copy-start | bytes 100
  3.0 5.7 %copy-start = (bf16[256,768]{1,0:T(8,128)(2,1)S(1)}, bf16[256,768]{1,0:T(8,128)(2,1)}, u32[]{:S(2)}) copy-start(bf16[256,768]{1,0:T(8,128)(2,1)} %param.11) | copy-start | bytes 1179652
  3.0 6.2 %copy-start.1 = (bf16[256,768]{1,0:T(8,128)(2,1)S(1)}, bf16[256,768]{1,0:T(8,128)(2,1)}, u32[]{:S(2)}) copy-start(bf16[256,768]{1,0:T(8,128)(2,1)} %param.9) | copy-start | bytes 1179652
  3.0 21.3 %all-to-all-start = ((bf16[8,528,128]{2,1,0:T(8,128)(2,1)}), bf16[8,528,128]{2,1,0:T(8,128)(2,1)S(1)}, u32[]{:S(2)}, u32[]{:S(2)}) async-start(bf16[8,528,128]{2,1,0:T(8,128)(2,1)} %pack.1), calls=%async_computation | async-start | bytes 2162688 | tf_op jit(solution)/shard_map/all_to_all | solution.py:365
  8.7 1.0 %copy-start.2 = (bf16[256,768]{1,0:T(8,128)(2,1)S(1)}, bf16[256,768]{1,0:T(8,128)(2,1)}, u32[]{:S(2)}) copy-start(bf16[256,768]{1,0:T(8,128)(2,1)} %param.10) | copy-start | bytes 1179652
  24.3 19.3 %all-to-all-start.1 = ((bf16[8,544,128]{2,1,0:T(8,128)(2,1)}), bf16[8,544,128]{2,1,0:T(8,128)(2,1)S(1)}, u32[]{:S(2)}, u32[]{:S(2)}) async-start(bf16[8,544,128]{2,1,0:T(8,128)(2,1)} %fusion.4), calls=%async_computation.1 | async-start | bytes 2228224 | tf_op jit(solution)/shard_map/all_to_all | solution.py:365
  27.9 2.0 %collective-permute-start = (bf16[8,272,128]{2,1,0:T(8,128)(2,1)S(1)}, bf16[8,272,128]{2,1,0:T(8,128)(2,1)S(1)}, u32[]{:S(2)}, u32[]{:S(2)}) collective-permute-start(bf16[8,272,128]{2,1,0:T(8,128)(2,1)S(1)} %slice.17), channel_id=1, source_target_pairs={{0,4},{4,0},{8,12},{12,8},{16,20},{20,16},{24,28},{28,24},{32,36},... | collective-permute-start | bytes 1671176 | tf_op jit(solution)/shard_map/ppermute | solution.py:381
  43.6 2.1 %collective-permute-start.1 = (bf16[8,288,128]{2,1,0:T(8,128)(2,1)S(1)}, bf16[8,288,128]{2,1,0:T(8,128)(2,1)S(1)}, u32[]{:S(2)}, u32[]{:S(2)}) collective-permute-start(bf16[8,288,128]{2,1,0:T(8,128)(2,1)S(1)} %slice.19), channel_id=1, source_target_pairs={{0,4},{4,0},{8,12},{12,8},{16,20},{20,16},{24,28},{28,24},{32,36},... | collective-permute-start | bytes 1769480 | tf_op jit(solution)/shard_map/ppermute | solution.py:392
  43.7 2.0 %collective-permute-start.2 = (f32[16,2,256]{2,1,0:T(2,128)S(1)}, f32[16,2,256]{2,1,0:T(2,128)S(1)}, u32[]{:S(2)}, u32[]{:S(2)}) collective-permute-start(f32[16,2,256]{2,1,0:T(2,128)S(1)} %prepare.1.stats_ref), channel_id=1, source_target_pairs={{0,4},{4,0},{8,12},{12,8},{16,20},{20,16},{24,28},{28,24},{32,36},... | collective-permute-start | bytes 98312 | tf_op jit(solution)/shard_map/ppermute | solution.py:390
  61.3 2.1 %collective-permute-start.3 = (bf16[9,256,128]{2,1,0:T(8,128)(2,1)S(1)}, bf16[9,256,128]{2,1,0:T(8,128)(2,1)S(1)}, u32[]{:S(2)}, u32[]{:S(2)}) collective-permute-start(bf16[9,256,128]{2,1,0:T(8,128)(2,1)S(1)} %get-tuple-element.15), channel_id=1, source_target_pairs={{0,4},{4,0},{8,12},{12,8},{16,20},{20,16},{24,28},{28,24},{32,36},... | collective-permute-start | bytes 1769480 | tf_op jit(solution)/shard_map/ppermute | solution.py:397

commit v4 on v3

--- a/solution.py
+++ b/solution.py
@@ -11,8 +11,8 @@
 QBLK = 128
 CHUNK = 256
 TILE = 2 * QBLK
-GROUP = 4
-WIDE = 6
+GROUP = 6
+RING = 3
 SCALE = HD ** (-0.5)
 RATE = SCALE * math.log2(math.e)
 FLOOR = -1e30
@@ -20,6 +20,7 @@
 
 smem = pl.BlockSpec(memory_space=pltpu.SMEM)
 vmem = pl.BlockSpec(memory_space=pltpu.VMEM)
+hbm = pl.BlockSpec(memory_space=pltpu.HBM)
 params = pltpu.CompilerParams(vmem_limit_bytes=32 * 1024 * 1024)
 small = pltpu.CompilerParams(vmem_limit_bytes=4 * 1024 * 1024)
 
@@ -86,39 +87,50 @@
     qt[HD : HD + EXTRA, rows] = jnp.where(within, FLOOR, 0.0).astype(jnp.bfloat16)
 
 
-def block_rows(block, base, size):
-    return pl.ds(pl.multiple_of(base + block % 2 * size, size), size)
-
-
-def fetch(own, other, block, base, size):
-    blocks = 2 * own.shape[0]
-    here = block % blocks
-    mine = own[here // 2, block_rows(here, CHUNK + base, size), :]
-    theirs = other[here // 2, block_rows(here, base, size), :]
-    return jnp.where(block < blocks, mine, theirs)
+def located(order_ref, token_block, chips):
+    at = order_ref[token_block]
+    mine = at < 2 * chips
+    here = jnp.where(mine, at, at - 2 * chips)
+    return mine, lax.div(here, 2), lax.rem(here, 2)
+
+
+def fetch(own, other, where, base, size):
+    mine, chip, half = where
+    here = own[chip, pl.ds(pl.multiple_of(CHUNK + base + half * size, size), size), :]
+    there = other[chip, pl.ds(pl.multiple_of(base + half * size, size), size), :]
+    return jnp.where(mine, here, there)
+
+
+def looped(count, unroll, body):
+    def several(i, carry):
+        for j in range(unroll):
+            body(unroll * i + j)
+        return carry
+
+    lax.fori_loop(0, count // unroll, several, 0)
 
 
 def prepare_kernel(
     core_ref, order_ref, units_ref, tile_ref, spot_ref, first_ref, other_ref, edges, sides,
-    stats_ref,
-    keys, qt, raw, tops, totals,
+    stats_ref, scores_ref,
+    keys, qt, raw, tops, totals, sems,
 ):
     core = core_ref[0]
     chips = first_ref.shape[0]
     tiles = stats_ref.shape[0]
 
-    def place(i, carry):
+    def place(i):
         place_key(keys, i, 2 * i + core, first_ref[i, :CHUNK, :], edges)
         for t in (2 * i, 2 * i + 1):
             for slot in range(2):
-                q = fetch(first_ref, other_ref, order_ref[2 * t + slot], 0, QBLK)
+                where = located(order_ref, 2 * t + slot, chips)
+                q = fetch(first_ref, other_ref, where, 0, QBLK)
                 place_query(qt.at[t], slot, q, (2 * t + slot) * QBLK, sides)
             qt[t, HD + EXTRA :, :] = jnp.zeros((HD - EXTRA, TILE), jnp.bfloat16)
             tops[t] = jnp.full((8, TILE), FLOOR, jnp.float32)
             totals[t] = jnp.zeros((8, TILE), jnp.float32)
-        return carry
-
-    lax.fori_loop(0, chips, place, 0)
+
+    looped(chips, 2, place)
     keys[chips] = jnp.ones((CHUNK, 2 * HD), jnp.bfloat16)
 
     def score(i, u):
@@ -127,15 +139,26 @@
     for u in range(GROUP):
         raw[0, u] = score(0, u)
 
+    def hand_over(i):
+        slot = i % RING
+        return pltpu.make_async_copy(raw.at[slot], scores_ref.at[i], sems.at[slot])
+
+    steps = (units_ref[0] + GROUP - 1) // GROUP
+
     def step(i, carry):
+        @pl.when(i >= RING - 1)
+        def _():
+            hand_over(i - (RING - 1)).wait()
+
+        hand_over(i).start()
         parts = []
         for u in range(GROUP):
-            s = raw[i % 2, u].reshape(4, 8, 8, TILE)
+            s = raw[i % RING, u].reshape(4, 8, 8, TILE)
             top = jnp.max(jnp.max(s, axis=1), axis=0)
             total = jnp.sum(jnp.sum(jnp.exp2((s - top) * RATE), axis=1), axis=0)
             parts.append((top, total))
         for u in range(GROUP):
-            raw[(i + 1) % 2, u] = score(i + 1, u)
+            raw[(i + 1) % RING, u] = score(i + 1, u)
         for u, (top, total) in enumerate(parts):
             t = tile_ref[GROUP * i + u]
             old = tops[t]
@@ -144,7 +167,7 @@
             tops[t] = new
         return carry
 
-    lax.fori_loop(0, (units_ref[0] + GROUP - 1) // GROUP, step, 0)
+    lax.fori_loop(0, steps, step, 0)
     for t in range(tiles):
         top = tops[t]
         row_top = jnp.max(top, axis=0, keepdims=True)
@@ -152,23 +175,32 @@
         stats_ref[t, 1:2] = jnp.sum(
             totals[t] * jnp.exp2((top - row_top) * RATE), axis=0, keepdims=True
         )
+    for back in range(RING - 1, 0, -1):
+        @pl.when(steps >= back)
+        def _():
+            hand_over(steps - back).wait()
 
 
 def prepare(scalars, first, other, edges, sides):
     chips = first.shape[0]
     tiles = 2 * chips
     pairs = tiles * TILE * 1024
+    steps = (tiles * chips + GROUP - 1) // GROUP
     return pl.pallas_call(
         prepare_kernel,
-        out_shape=jax.ShapeDtypeStruct((tiles, 2, TILE), jnp.float32),
+        out_shape=(
+            jax.ShapeDtypeStruct((tiles, 2, TILE), jnp.float32),
+            jax.ShapeDtypeStruct((steps, GROUP, CHUNK, TILE), jnp.float32),
+        ),
         in_specs=[smem] * len(scalars) + [vmem] * 4,
-        out_specs=vmem,
+        out_specs=(vmem, hbm),
         scratch_shapes=[
             pltpu.VMEM((chips + 1, CHUNK, 2 * HD), jnp.bfloat16),
             pltpu.VMEM((tiles, 2 * HD, TILE), jnp.bfloat16),
-            pltpu.VMEM((2, GROUP, CHUNK, TILE), jnp.float32),
+            pltpu.VMEM((RING, GROUP, CHUNK, TILE), jnp.float32),
             pltpu.VMEM((tiles, 8, TILE), jnp.float32),
             pltpu.VMEM((tiles, 8, TILE), jnp.float32),
+            pltpu.SemaphoreType.DMA((RING,)),
         ],
         compiler_params=params,
         cost_estimate=pl.CostEstimate(
@@ -179,18 +211,32 @@
 
 
 def grads_kernel(
-    core_ref, order_ref, units_ref, tile_ref, spot_ref, first_ref, other_ref, edges, sides,
-    second_ref, second_other, stats_ref, stats_other,
+    core_ref, order_ref, units_ref, tile_ref, spot_ref, first_ref, other_ref,
+    second_ref, second_other, stats_ref, stats_other, scores_ref,
     keep_ref, send_ref, dkv_ref,
-    keys, keys_t, values, qs, qt, gs, gt, level, raw, slope, acc_k, acc_v, acc_q,
+    keys_t, values, qs, gs, gt, level, raw, slope, acc_k, acc_v, acc_q, sems,
 ):
-    core = core_ref[0]
     chips = first_ref.shape[0]
-
-    def place(i, carry):
-        k = first_ref[i, :CHUNK, :]
-        place_key(keys, i, 2 * i + core, k, edges)
-        keys_t[i] = k.T
+    steps = (units_ref[0] + GROUP - 1) // GROUP
+
+    def take_over(i):
+        slot = i % RING
+        return [
+            pltpu.make_async_copy(scores_ref.at[i, u], raw.at[slot, u], sems.at[slot, u])
+            for u in range(GROUP)
+        ]
+
+    def begin(i):
+        @pl.when(i < steps)
+        def _():
+            for copy in take_over(i):
+                copy.start()
+
+    for i in range(RING - 1):
+        begin(i)
+
+    def place(i):
+        keys_t[i] = first_ref[i, :CHUNK, :].T
         values[i, :, :HD] = second_ref[i, :CHUNK, :]
         values[i, :, HD:] = jnp.full((CHUNK, HD), -1, jnp.bfloat16)
         acc_k[i] = jnp.zeros((CHUNK, HD), jnp.float32)
@@ -198,17 +244,16 @@
         for t in (2 * i, 2 * i + 1):
             acc_q[t] = jnp.zeros((HD, TILE), jnp.float32)
             for slot in range(2):
-                block = order_ref[2 * t + slot]
                 rows = slice(slot * QBLK, (slot + 1) * QBLK)
-                q = fetch(first_ref, other_ref, block, 0, QBLK)
-                g = fetch(second_ref, second_other, block, 0, QBLK)
+                where = located(order_ref, 2 * t + slot, chips)
+                q = fetch(first_ref, other_ref, where, 0, QBLK)
+                g = fetch(second_ref, second_other, where, 0, QBLK)
                 qs[t, rows, :] = q
                 gs[t, rows, :] = g
-                place_query(qt.at[t], slot, q, (2 * t + slot) * QBLK, sides)
                 gt[t, :HD, rows] = g.T
-                gt[t, HD : HD + EXTRA, rows] = fetch(second_ref, second_other, block, CHUNK, EXTRA)
-            for ref in (qt, gt):
-                ref[t, HD + EXTRA :, :] = jnp.zeros((HD - EXTRA, TILE), jnp.bfloat16)
+                delta = fetch(second_ref, second_other, where, CHUNK, EXTRA)
+                gt[t, HD : HD + EXTRA, rows] = delta
+            gt[t, HD + EXTRA :, :] = jnp.zeros((HD - EXTRA, TILE), jnp.bfloat16)
             tops = [ref[t, 0:1] for ref in (stats_ref, stats_other)]
             top = jnp.maximum(*tops)
             total = sum(
@@ -216,30 +261,30 @@
                 for x, ref in zip(tops, (stats_ref, stats_other))
             )
             level[t] = top + jnp.log2(total) * (1.0 / RATE)
-        return carry
-
-    lax.fori_loop(0, chips, place, 0)
-    keys[chips] = jnp.ones((CHUNK, 2 * HD), jnp.bfloat16)
+
+    looped(chips, 2, place)
     keys_t[chips] = jnp.zeros((HD, CHUNK), jnp.bfloat16)
     values[chips] = jnp.zeros((CHUNK, 2 * HD), jnp.bfloat16)
     acc_k[chips] = jnp.zeros((CHUNK, HD), jnp.float32)
     acc_v[chips] = jnp.zeros((CHUNK, HD), jnp.float32)
 
     def unit(i, u):
-        return tile_ref[WIDE * i + u], spot_ref[WIDE * i + u]
+        return tile_ref[GROUP * i + u], spot_ref[GROUP * i + u]
 
     def ahead(i):
-        for u in range(WIDE):
+        for u in range(GROUP):
             t, spot = unit(i, u)
-            raw[i % 2, u] = dot(keys[spot], qt[t])
             slope[i % 2, u] = dot(values[spot], gt[t])
 
     ahead(0)
 
     def work(i):
-        for u in range(WIDE):
+        for copy in take_over(i):
+            copy.wait()
+        begin(i + RING - 1)
+        for u in range(GROUP):
             t, spot = unit(i, u)
-            p = jnp.exp2((raw[i % 2, u] - level[t]) * RATE)
+            p = jnp.exp2((raw[i % RING, u] - level[t]) * RATE)
             s = (p * slope[i % 2, u]).astype(jnp.bfloat16)
             acc_v[spot] += dot(p.astype(jnp.bfloat16), gs[t])
             acc_k[spot] += dot(s, qs[t])
@@ -250,29 +295,25 @@
         ahead(i + 1)
         return carry
 
-    last = (units_ref[0] + WIDE - 1) // WIDE - 1
-    lax.fori_loop(0, last, step, 0)
-    work(last)
-
-    def hand_out(i, carry):
+    lax.fori_loop(0, steps - 1, step, 0)
+    work(steps - 1)
+
+    def hand_out(i):
         dkv_ref[i, :CHUNK] = (acc_k[i] * SCALE).astype(jnp.bfloat16)
         dkv_ref[i, CHUNK:] = acc_v[i].astype(jnp.bfloat16)
         for t in (2 * i, 2 * i + 1):
             result = (acc_q[t] * SCALE).T
             for slot in range(2):
-                block = order_ref[2 * t + slot]
-                here = block % (2 * chips)
-                rows = block_rows(here, 0, QBLK)
+                mine, chip, half = located(order_ref, 2 * t + slot, chips)
+                rows = pl.ds(pl.multiple_of(half * QBLK, QBLK), QBLK)
                 part = result[slot * QBLK : (slot + 1) * QBLK]
-                mine = block < 2 * chips
-                keep_ref[jnp.where(mine, here // 2, chips), rows, :] = part
-                send_ref[jnp.where(mine, chips, here // 2), rows, :] = part.astype(jnp.bfloat16)
-        return carry
-
-    lax.fori_loop(0, chips, hand_out, 0)
-
-
-def grads(scalars, first, other, edges, sides, second, second_other, stats, stats_other):
+                keep_ref[jnp.where(mine, chip, chips), rows, :] = part
+                send_ref[jnp.where(mine, chips, chip), rows, :] = part.astype(jnp.bfloat16)
+
+    looped(chips, 2, hand_out)
+
+
+def grads(scalars, first, other, second, second_other, stats, stats_other, scores):
     chips = second.shape[0]
     tiles = 2 * chips
     pairs = tiles * TILE * 1024
@@ -284,29 +325,28 @@
             jax.ShapeDtypeStruct((chips + 1, TILE, HD), bf16),
             jax.ShapeDtypeStruct((chips, 2 * CHUNK, HD), bf16),
         ),
-        in_specs=[smem] * len(scalars) + [vmem] * 8,
+        in_specs=[smem] * len(scalars) + [vmem] * 6 + [hbm],
         out_specs=(vmem,) * 3,
         scratch_shapes=[
-            pltpu.VMEM((chips + 1, CHUNK, 2 * HD), bf16),
             pltpu.VMEM((chips + 1, HD, CHUNK), bf16),
             pltpu.VMEM((chips + 1, CHUNK, 2 * HD), bf16),
             pltpu.VMEM((tiles, TILE, HD), bf16),
-            pltpu.VMEM((tiles, 2 * HD, TILE), bf16),
             pltpu.VMEM((tiles, TILE, HD), bf16),
             pltpu.VMEM((tiles, 2 * HD, TILE), bf16),
             pltpu.VMEM((tiles, 1, TILE), f32),
-            pltpu.VMEM((2, WIDE, CHUNK, TILE), f32),
-            pltpu.VMEM((2, WIDE, CHUNK, TILE), f32),
+            pltpu.VMEM((RING, GROUP, CHUNK, TILE), f32),
+            pltpu.VMEM((2, GROUP, CHUNK, TILE), f32),
             pltpu.VMEM((chips + 1, CHUNK, HD), f32),
             pltpu.VMEM((chips + 1, CHUNK, HD), f32),
             pltpu.VMEM((tiles, HD, TILE), f32),
+            pltpu.SemaphoreType.DMA((RING, GROUP)),
         ],
         compiler_params=params,
         cost_estimate=pl.CostEstimate(
             flops=10 * pairs * HD, bytes_accessed=10 * 2**20, transcendentals=pairs
         ),
         name="grads",
-    )(*scalars, first, other, edges, sides, second, second_other, stats, stats_other)
+    )(*scalars, first, other, second, second_other, stats, stats_other, scores)
 
 
 def plan(lengths, core, chips):
@@ -325,7 +365,7 @@
     needed = needed.astype(jnp.int32).reshape(-1)
     cells = jnp.arange(needed.shape[0], dtype=jnp.int32)
     before = jnp.sum(needed[None, :] * (cells[None, :] < cells[:, None]), axis=1)
-    slots = jnp.arange(needed.shape[0] + 2 * max(GROUP, WIDE), dtype=jnp.int32)
+    slots = jnp.arange(needed.shape[0] + 2 * GROUP, dtype=jnp.int32)
     chosen = (before[None, :] == slots[:, None]) & (needed[None, :] > 0)
     cell = jnp.sum(jnp.where(chosen, cells[None, :], 0), axis=1)
     total = jnp.sum(needed, keepdims=True)
@@ -386,12 +426,12 @@
     units, tile, spot = plan(lengths, core, chips)
     scalars = (jnp.full((1,), core, jnp.int32), order, units, tile, spot)
     edges, sides = edges_of(lengths, size * rows)
-    stats = prepare(scalars, first, other, edges, sides)
+    stats, scores = prepare(scalars, first, other, edges, sides)
     stats_other = lax.ppermute(stats, "seq", swap)
     second, stats = lax.optimization_barrier((second, stats))
     second_other = lax.ppermute(second[:, rows:], "seq", swap)
     keep, send, dkv = grads(
-        scalars, first, other, edges, sides, second, second_other, stats, stats_other
+        scalars, first, other, second, second_other, stats, stats_other, scores
     )
 
     received = lax.ppermute(send, "seq", swap)

time: 89.7 us -> 87 us (0.970)
  Pallas kernels: 28.8 us -> 25.7 us
    pallas_call x1, Pallas kernels: 15.5 us -> 13.1 us  [grads(): pl.pallas_call(grads_kernel, out_shape=(jax.ShapeDtypeStruct((chips + 1,...]
where the time goes in v4:
time: 87 us; the launch traced here: 86.6 us
  Pallas kernels  25.7 us (30%)
  blocking collectives  24.3 us (28%)
  waiting for transfers between devices  20.5 us (24%)
  starting transfers between devices  9.68 us (11%)
  other arithmetic  3.77 us (4%)
  local copies, waits for them, and re-layouts  1.78 us (2%)
    all_to_all x1, blocking collectives, exchange(): return lax.all_to_all(x, 'seq', 0, 0, axis_index_groups=groups)  24.3 us
    all_to_all x2, waiting for transfers between devices, exchange(): return lax.all_to_all(x, 'seq', 0, 0, axis_index_groups=groups)  16.8 us
    pallas_call x1, Pallas kernels, grads(): pl.pallas_call(grads_kernel, out_shape=(jax.ShapeDtypeStruct((chips + 1,...  13.1 us
    pallas_call x1, Pallas kernels, prepare(): pl.pallas_call(prepare_kernel, out_shape=(jax.ShapeDtypeStruct((tiles, 2,...  9.16 us
    all_to_all x2, starting transfers between devices, exchange(): return lax.all_to_all(x, 'seq', 0, 0, axis_index_groups=groups)  8.8 us
    pallas_call x1, Pallas kernels, pack(): pl.pallas_call(pack_kernel, out_shape=jax.ShapeDtypeStruct((chips, 2 * ro...  2.3 us
    ppermute x1, waiting for transfers between devices, on_device(): received = lax.ppermute(send, 'seq', swap)  1.87 us
  transfers between devices with their start and end apart: 6, of which 5 were waited for; matrix products, arithmetic and copies ran while one was open for 6% of the time, Pallas kernels for 11%

profile of v4, /device:TPU:4, one launch (start us, length us, event | category | flops | bytes accessed | tf_op | source)
XLA Modules:
  0.0 86.6 jit_solution(857713450585551860)
XLA Ops:
  0.6 2.3 %pack.1 = bf16[8,528,128]{2,1,0:T(8,128)(2,1)} custom-call(s32[2]{0:T(128)} %ids_ref.1, bf16[256,768]{1,0:T(8,128)(2,1)} %k_ref.1, bf16[256,768]{1,0:T(8,128)(2,1)} %q_ref.1), custom_call_target="tpu_custom_call" | custom-call | tf_op jit(solution)/shard_map/pack/pallas_call | solution.py:46
  2.9 5.2 %all-to-all-start = ((bf16[8,528,128]{2,1,0:T(8,128)(2,1)}), bf16[8,528,128]{2,1,0:T(8,128)(2,1)S(1)}, u32[]{:S(2)}, u32[]{:S(2)}) async-start(bf16[8,528,128]{2,1,0:T(8,128)(2,1)} %pack.1), calls=%async_computation | async-start | bytes 2162688 | tf_op jit(solution)/shard_map/all_to_all | solution.py:405
  8.2 0.2 reduce-window.8
  8.7 0.2 copy.24
  8.9 0.2 copy.25
  9.1 0.2 copy.22
  9.3 0.2 copy.23
  9.5 0.2 copy-done.2
  9.7 0.2 copy.27
  10.1 0.1 select_reduce_fusion.1
  10.2 1.1 %fusion.4 = bf16[8,544,128]{2,1,0:T(8,128)(2,1)} fusion(bf16[6,32,128]{2,1,0:T(8,128)(2,1)S(1)} %bitcast.23, bf16[6,256,128]{2,1,0:T(8,128)(2,1)S(1)} %bitcast.21, bf16[6,256,128]{2,1,0:T(8,128)(2,1)S(1)} %bitcast.22), kind=kLoop, calls=%fused_computation.6 | loop fusion | flops 5570560 | bytes 1949696 | tf_op jit(solution)/shard_map/concatenate | solution.py:416
  11.4 12.9 %all-to-all-done.first_ref = bf16[8,528,128]{2,1,0:T(8,128)(2,1)S(1)} async-done(((bf16[8,528,128]{2,1,0:T(8,128)(2,1)}), bf16[8,528,128]{2,1,0:T(8,128)(2,1)S(1)}, u32[]{:S(2)}, u32[]{:S(2)}) %all-to-all-start) | async-done | bytes 1081376 | tf_op jit(solution)/shard_map/all_to_all | solution.py:405
  24.2 3.6 %all-to-all-start.1 = ((bf16[8,544,128]{2,1,0:T(8,128)(2,1)}), bf16[8,544,128]{2,1,0:T(8,128)(2,1)S(1)}, u32[]{:S(2)}, u32[]{:S(2)}) async-start(bf16[8,544,128]{2,1,0:T(8,128)(2,1)} %fusion.4), calls=%async_computation.1 | async-start | bytes 2228224 | tf_op jit(solution)/shard_map/all_to_all | solution.py:405
  28.0 0.1 select_reduce_fusion
  28.1 0.7 fusion.14
  28.8 0.7 compare_select_fusion.2
  29.5 0.1 copy.28
  29.6 0.3 collective-permute-done.other_ref
  29.9 0.1 copy.29
  30.2 0.1 reshape.214
  30.3 0.1 select_reduce_fusion.2.order_ref
  30.4 9.2 %prepare.1 = (f32[16,2,256]{2,1,0:T(2,128)S(1)}, f32[22,6,256,256]{3,2,1,0:T(8,128)}) custom-call(s32[1]{0:T(128)} %bitcast.core_ref, s32[32]{0:T(128)S(1)} %select_reduce_fusion.2.order_ref, s32[1]{0:T(128)} %bitcast.12.units_ref, s32[140]{0:T(256)S(1)} %get-tuple-element.27.tile_ref, s32[140]{0:T(256)S(1)} %get-tuple-element.26.spot_ref, ...), custom_call_target="tpu_custom_call" | custom-call | flops 2147483648 | bytes 8388608 | tf_op jit(solution)/shard_map/prepare/pallas_call | solution.py:189
  39.6 3.9 %all-to-all-done.1.second_ref = bf16[8,544,128]{2,1,0:T(8,128)(2,1)S(1)} async-done(((bf16[8,544,128]{2,1,0:T(8,128)(2,1)}), bf16[8,544,128]{2,1,0:T(8,128)(2,1)S(1)}, u32[]{:S(2)}, u32[]{:S(2)}) %all-to-all-start.1) | async-done | bytes 1114144 | tf_op jit(solution)/shard_map/all_to_all | solution.py:405
  43.7 0.5 collective-permute-start.2
  44.2 1.5 %collective-permute-done.2.stats_other = f32[16,2,256]{2,1,0:T(2,128)S(1)} collective-permute-done((f32[16,2,256]{2,1,0:T(2,128)S(1)}, f32[16,2,256]{2,1,0:T(2,128)S(1)}, u32[]{:S(2)}, u32[]{:S(2)}) %collective-permute-start.2) | collective-permute-done | bytes 32800 | tf_op jit(solution)/shard_map/ppermute | solution.py:430
  45.7 13.1 %grads.1 = (f32[9,256,128]{2,1,0:T(8,128)S(1)}, bf16[9,256,128]{2,1,0:T(8,128)(2,1)S(1)}, bf16[8,512,128]{2,1,0:T(8,128)(2,1)S(1)}) custom-call(s32[1]{0:T(128)} %bitcast.core_ref, s32[32]{0:T(128)S(1)} %select_reduce_fusion.2.order_ref, s32[1]{0:T(128)} %bitcast.12.units_ref, s32[140]{0:T(256)S(1)} %get-tuple-element.27.tile_ref, ...), custom_call_target="tpu_custom_call" | custom-call | flops 5368709120 | bytes 10485760 | tf_op jit(solution)/shard_map/grads/pallas_call | solution.py:321
  58.8 0.2 collective-permute-start.3
  59.0 1.9 %collective-permute-done.3 = bf16[9,256,128]{2,1,0:T(8,128)(2,1)S(1)} collective-permute-done((bf16[9,256,128]{2,1,0:T(8,128)(2,1)S(1)}, bf16[9,256,128]{2,1,0:T(8,128)(2,1)S(1)}, u32[]{:S(2)}, u32[]{:S(2)}) %collective-permute-start.3) | collective-permute-done | bytes 589856 | tf_op jit(solution)/shard_map/ppermute | solution.py:437
  60.9 0.1 fusion.5
  61.0 0.1 pad_maximum_fusion
  61.1 24.3 %all_to_all.15.x_ref = bf16[8,768,128]{2,1,0:T(8,128)(2,1)S(1)} all-to-all(bf16[8,768,128]{2,1,0:T(8,128)(2,1)S(1)} %pad_maximum_fusion), channel_id=1, replica_groups={{0,8,16,24,32,40,48,56},{4,12,20,28,36,44,52,60},{1,9,17,25,33,41,49,57..., dimensions={0} | all-to-all | bytes 3145728 | tf_op jit(solution)/shard_map/all_to_all | solution.py:405
  85.4 1.2 %unpack.1 = (bf16[256,768]{1,0:T(8,128)(2,1)}, bf16[256,768]{1,0:T(8,128)(2,1)}, bf16[256,768]{1,0:T(8,128)(2,1)}) custom-call(bf16[8,768,128]{2,1,0:T(8,128)(2,1)S(1)} %all_to_all.15.x_ref), custom_call_target="tpu_custom_call" | custom-call | tf_op jit(solution)/shard_map/unpack/pallas_call | solution.py:65
  (34 shorter events, 1.1 us)
Async XLA Ops:
  0.6 7.6 %copy-start.3 = (s32[8]{0:T(128)S(1)}, s32[8]{0:T(128)}, u32[]{:S(2)}) copy-start(s32[8]{0:T(128)} %param.12) | copy-start | bytes 100
  2.9 5.7 %copy-start = (bf16[256,768]{1,0:T(8,128)(2,1)S(1)}, bf16[256,768]{1,0:T(8,128)(2,1)}, u32[]{:S(2)}) copy-start(bf16[256,768]{1,0:T(8,128)(2,1)} %param.11) | copy-start | bytes 1179652
  2.9 6.2 %copy-start.1 = (bf16[256,768]{1,0:T(8,128)(2,1)S(1)}, bf16[256,768]{1,0:T(8,128)(2,1)}, u32[]{:S(2)}) copy-start(bf16[256,768]{1,0:T(8,128)(2,1)} %param.9) | copy-start | bytes 1179652
  2.9 21.3 %all-to-all-start = ((bf16[8,528,128]{2,1,0:T(8,128)(2,1)}), bf16[8,528,128]{2,1,0:T(8,128)(2,1)S(1)}, u32[]{:S(2)}, u32[]{:S(2)}) async-start(bf16[8,528,128]{2,1,0:T(8,128)(2,1)} %pack.1), calls=%async_computation | async-start | bytes 2162688 | tf_op jit(solution)/shard_map/all_to_all | solution.py:405
  8.7 1.0 %copy-start.2 = (bf16[256,768]{1,0:T(8,128)(2,1)S(1)}, bf16[256,768]{1,0:T(8,128)(2,1)}, u32[]{:S(2)}) copy-start(bf16[256,768]{1,0:T(8,128)(2,1)} %param.10) | copy-start | bytes 1179652
  24.2 19.3 %all-to-all-start.1 = ((bf16[8,544,128]{2,1,0:T(8,128)(2,1)}), bf16[8,544,128]{2,1,0:T(8,128)(2,1)S(1)}, u32[]{:S(2)}, u32[]{:S(2)}) async-start(bf16[8,544,128]{2,1,0:T(8,128)(2,1)} %fusion.4), calls=%async_computation.1 | async-start | bytes 2228224 | tf_op jit(solution)/shard_map/all_to_all | solution.py:405
  27.8 2.0 %collective-permute-start = (bf16[8,272,128]{2,1,0:T(8,128)(2,1)S(1)}, bf16[8,272,128]{2,1,0:T(8,128)(2,1)S(1)}, u32[]{:S(2)}, u32[]{:S(2)}) collective-permute-start(bf16[8,272,128]{2,1,0:T(8,128)(2,1)S(1)} %slice.17), channel_id=1, source_target_pairs={{0,4},{4,0},{8,12},{12,8},{16,20},{20,16},{24,28},{28,24},{32,36},... | collective-permute-start | bytes 1671176 | tf_op jit(solution)/shard_map/ppermute | solution.py:421
  43.6 2.1 %collective-permute-start.1 = (bf16[8,288,128]{2,1,0:T(8,128)(2,1)S(1)}, bf16[8,288,128]{2,1,0:T(8,128)(2,1)S(1)}, u32[]{:S(2)}, u32[]{:S(2)}) collective-permute-start(bf16[8,288,128]{2,1,0:T(8,128)(2,1)S(1)} %slice.19), channel_id=1, source_target_pairs={{0,4},{4,0},{8,12},{12,8},{16,20},{20,16},{24,28},{28,24},{32,36},... | collective-permute-start | bytes 1769480 | tf_op jit(solution)/shard_map/ppermute | solution.py:432
  43.7 2.0 %collective-permute-start.2 = (f32[16,2,256]{2,1,0:T(2,128)S(1)}, f32[16,2,256]{2,1,0:T(2,128)S(1)}, u32[]{:S(2)}, u32[]{:S(2)}) collective-permute-start(f32[16,2,256]{2,1,0:T(2,128)S(1)} %get-tuple-element.16.stats_ref), channel_id=1, source_target_pairs={{0,4},{4,0},{8,12},{12,8},{16,20},{20,16},{24,28},{28,24},{32,36},... | collective-permute-start | bytes 98312 | tf_op jit(solution)/shard_map/ppermute | solution.py:430
  58.8 2.1 %collective-permute-start.3 = (bf16[9,256,128]{2,1,0:T(8,128)(2,1)S(1)}, bf16[9,256,128]{2,1,0:T(8,128)(2,1)S(1)}, u32[]{:S(2)}, u32[]{:S(2)}) collective-permute-start(bf16[9,256,128]{2,1,0:T(8,128)(2,1)S(1)} %get-tuple-element.19), channel_id=1, source_target_pairs={{0,4},{4,0},{8,12},{12,8},{16,20},{20,16},{24,28},{28,24},{32,36},... | collective-permute-start | bytes 1769480 | tf_op jit(solution)/shard_map/ppermute | solution.py:437

commit v5 on v4

--- a/solution.py
+++ b/solution.py
@@ -130,7 +130,7 @@
             tops[t] = jnp.full((8, TILE), FLOOR, jnp.float32)
             totals[t] = jnp.zeros((8, TILE), jnp.float32)
 
-    looped(chips, 2, place)
+    looped(chips, 4, place)
     keys[chips] = jnp.ones((CHUNK, 2 * HD), jnp.bfloat16)
 
     def score(i, u):
@@ -214,7 +214,7 @@
     core_ref, order_ref, units_ref, tile_ref, spot_ref, first_ref, other_ref,
     second_ref, second_other, stats_ref, stats_other, scores_ref,
     keep_ref, send_ref, dkv_ref,
-    keys_t, values, qs, gs, gt, level, raw, slope, acc_k, acc_v, acc_q, sems,
+    keys_t, values, qs, gs, gt, level, raw, acc_k, acc_v, acc_q, sems,
 ):
     chips = first_ref.shape[0]
     steps = (units_ref[0] + GROUP - 1) // GROUP
@@ -262,7 +262,7 @@
             )
             level[t] = top + jnp.log2(total) * (1.0 / RATE)
 
-    looped(chips, 2, place)
+    looped(chips, 4, place)
     keys_t[chips] = jnp.zeros((HD, CHUNK), jnp.bfloat16)
     values[chips] = jnp.zeros((CHUNK, 2 * HD), jnp.bfloat16)
     acc_k[chips] = jnp.zeros((CHUNK, HD), jnp.float32)
@@ -271,32 +271,41 @@
     def unit(i, u):
         return tile_ref[GROUP * i + u], spot_ref[GROUP * i + u]
 
-    def ahead(i):
-        for u in range(GROUP):
-            t, spot = unit(i, u)
-            slope[i % 2, u] = dot(values[spot], gt[t])
-
-    ahead(0)
-
     def work(i):
         for copy in take_over(i):
             copy.wait()
         begin(i + RING - 1)
-        for u in range(GROUP):
-            t, spot = unit(i, u)
+        units = [unit(i, u) for u in range(GROUP)]
+        slopes = {}
+        lows = {}
+
+        def slope(u):
+            if u < GROUP:
+                t, spot = units[u]
+                slopes[u] = dot(values[spot], gt[t])
+
+        def finish(u):
+            if 0 <= u < GROUP:
+                t, spot = units[u]
+                acc_k[spot] += dot(lows[u], qs[t])
+                acc_q[t] += dot(keys_t[spot], lows[u])
+
+        for u in range(2):
+            slope(u)
+        for u, (t, spot) in enumerate(units):
             p = jnp.exp2((raw[i % RING, u] - level[t]) * RATE)
-            s = (p * slope[i % 2, u]).astype(jnp.bfloat16)
+            slope(u + 2)
             acc_v[spot] += dot(p.astype(jnp.bfloat16), gs[t])
-            acc_k[spot] += dot(s, qs[t])
-            acc_q[t] += dot(keys_t[spot], s)
+            lows[u] = (p * slopes[u]).astype(jnp.bfloat16)
+            finish(u - 1)
+        for u in range(GROUP - 1, GROUP):
+            finish(u)
 
     def step(i, carry):
         work(i)
-        ahead(i + 1)
         return carry
 
-    lax.fori_loop(0, steps - 1, step, 0)
-    work(steps - 1)
+    lax.fori_loop(0, steps, step, 0)
 
     def hand_out(i):
         dkv_ref[i, :CHUNK] = (acc_k[i] * SCALE).astype(jnp.bfloat16)
@@ -310,7 +319,7 @@
                 keep_ref[jnp.where(mine, chip, chips), rows, :] = part
                 send_ref[jnp.where(mine, chips, chip), rows, :] = part.astype(jnp.bfloat16)
 
-    looped(chips, 2, hand_out)
+    looped(chips, 4, hand_out)
 
 
 def grads(scalars, first, other, second, second_other, stats, stats_other, scores):
@@ -335,7 +344,6 @@
             pltpu.VMEM((tiles, 2 * HD, TILE), bf16),
             pltpu.VMEM((tiles, 1, TILE), f32),
             pltpu.VMEM((RING, GROUP, CHUNK, TILE), f32),
-            pltpu.VMEM((2, GROUP, CHUNK, TILE), f32),
             pltpu.VMEM((chips + 1, CHUNK, HD), f32),
             pltpu.VMEM((chips + 1, CHUNK, HD), f32),
             pltpu.VMEM((tiles, HD, TILE), f32),

time: 87 us -> 87.1 us (level)
  no operation moved by 1% of the time
where the time goes in v5:
time: 87.1 us; the launch traced here: 86.3 us
  Pallas kernels  25.3 us (29%)
  blocking collectives  24.3 us (28%)
  waiting for transfers between devices  20.7 us (24%)
  starting transfers between devices  9.55 us (11%)
  other arithmetic  3.77 us (4%)
  local copies, waits for them, and re-layouts  1.78 us (2%)
    all_to_all x1, blocking collectives, exchange(): return lax.all_to_all(x, 'seq', 0, 0, axis_index_groups=groups)  24.3 us
    all_to_all x2, waiting for transfers between devices, exchange(): return lax.all_to_all(x, 'seq', 0, 0, axis_index_groups=groups)  16.9 us
    pallas_call x1, Pallas kernels, grads(): pl.pallas_call(grads_kernel, out_shape=(jax.ShapeDtypeStruct((chips + 1,...  12.7 us
    pallas_call x1, Pallas kernels, prepare(): pl.pallas_call(prepare_kernel, out_shape=(jax.ShapeDtypeStruct((tiles, 2,...  9.09 us
    all_to_all x2, starting transfers between devices, exchange(): return lax.all_to_all(x, 'seq', 0, 0, axis_index_groups=groups)  8.8 us
    pallas_call x1, Pallas kernels, pack(): pl.pallas_call(pack_kernel, out_shape=jax.ShapeDtypeStruct((chips, 2 * ro...  2.3 us
    ppermute x1, waiting for transfers between devices, on_device(): received = lax.ppermute(send, 'seq', swap)  1.99 us
  transfers between devices with their start and end apart: 6, of which 5 were waited for; matrix products, arithmetic and copies ran while one was open for 6% of the time, Pallas kernels for 11%

profile of v5, /device:TPU:4, one launch (start us, length us, event | category | flops | bytes accessed | tf_op | source)
XLA Modules:
  0.0 86.3 jit_solution(8760888696440306617)
XLA Ops:
  0.6 2.3 %pack.1 = bf16[8,528,128]{2,1,0:T(8,128)(2,1)} custom-call(s32[2]{0:T(128)} %ids_ref.1, bf16[256,768]{1,0:T(8,128)(2,1)} %k_ref.1, bf16[256,768]{1,0:T(8,128)(2,1)} %q_ref.1), custom_call_target="tpu_custom_call" | custom-call | tf_op jit(solution)/shard_map/pack/pallas_call | solution.py:46
  2.9 5.2 %all-to-all-start = ((bf16[8,528,128]{2,1,0:T(8,128)(2,1)}), bf16[8,528,128]{2,1,0:T(8,128)(2,1)S(1)}, u32[]{:S(2)}, u32[]{:S(2)}) async-start(bf16[8,528,128]{2,1,0:T(8,128)(2,1)} %pack.1), calls=%async_computation | async-start | bytes 2162688 | tf_op jit(solution)/shard_map/all_to_all | solution.py:413
  8.2 0.2 reduce-window.8
  8.6 0.1 reshape.215
  8.7 0.2 copy.24
  8.9 0.2 copy.25
  9.1 0.2 copy.22
  9.3 0.2 copy.23
  9.5 0.2 copy-done.2
  9.7 0.2 copy.27
  10.1 0.1 select_reduce_fusion.1
  10.2 1.1 %fusion.4 = bf16[8,544,128]{2,1,0:T(8,128)(2,1)} fusion(bf16[6,32,128]{2,1,0:T(8,128)(2,1)S(1)} %bitcast.23, bf16[6,256,128]{2,1,0:T(8,128)(2,1)S(1)} %bitcast.21, bf16[6,256,128]{2,1,0:T(8,128)(2,1)S(1)} %bitcast.22), kind=kLoop, calls=%fused_computation.6 | loop fusion | flops 5570560 | bytes 1949696 | tf_op jit(solution)/shard_map/concatenate | solution.py:424
  11.4 12.9 %all-to-all-done.first_ref = bf16[8,528,128]{2,1,0:T(8,128)(2,1)S(1)} async-done(((bf16[8,528,128]{2,1,0:T(8,128)(2,1)}), bf16[8,528,128]{2,1,0:T(8,128)(2,1)S(1)}, u32[]{:S(2)}, u32[]{:S(2)}) %all-to-all-start) | async-done | bytes 1081376 | tf_op jit(solution)/shard_map/all_to_all | solution.py:413
  24.2 3.6 %all-to-all-start.1 = ((bf16[8,544,128]{2,1,0:T(8,128)(2,1)}), bf16[8,544,128]{2,1,0:T(8,128)(2,1)S(1)}, u32[]{:S(2)}, u32[]{:S(2)}) async-start(bf16[8,544,128]{2,1,0:T(8,128)(2,1)} %fusion.4), calls=%async_computation.1 | async-start | bytes 2228224 | tf_op jit(solution)/shard_map/all_to_all | solution.py:413
  28.0 0.1 select_reduce_fusion
  28.1 0.7 fusion.14
  28.8 0.7 compare_select_fusion.2
  29.5 0.1 copy.28
  29.6 0.3 collective-permute-done.other_ref
  29.9 0.1 copy.29
  30.2 0.1 reshape.214
  30.3 0.1 select_reduce_fusion.2.order_ref
  30.4 9.1 %prepare.1 = (f32[16,2,256]{2,1,0:T(2,128)S(1)}, f32[22,6,256,256]{3,2,1,0:T(8,128)}) custom-call(s32[1]{0:T(128)} %bitcast.core_ref, s32[32]{0:T(128)S(1)} %select_reduce_fusion.2.order_ref, s32[1]{0:T(128)} %bitcast.12.units_ref, s32[140]{0:T(256)S(1)} %get-tuple-element.27.tile_ref, s32[140]{0:T(256)S(1)} %get-tuple-element.26.spot_ref, ...), custom_call_target="tpu_custom_call" | custom-call | flops 2147483648 | bytes 8388608 | tf_op jit(solution)/shard_map/prepare/pallas_call | solution.py:189
  39.5 4.0 %all-to-all-done.1.second_ref = bf16[8,544,128]{2,1,0:T(8,128)(2,1)S(1)} async-done(((bf16[8,544,128]{2,1,0:T(8,128)(2,1)}), bf16[8,544,128]{2,1,0:T(8,128)(2,1)S(1)}, u32[]{:S(2)}, u32[]{:S(2)}) %all-to-all-start.1) | async-done | bytes 1114144 | tf_op jit(solution)/shard_map/all_to_all | solution.py:413
  43.7 0.5 collective-permute-start.2
  44.2 1.5 %collective-permute-done.2.stats_other = f32[16,2,256]{2,1,0:T(2,128)S(1)} collective-permute-done((f32[16,2,256]{2,1,0:T(2,128)S(1)}, f32[16,2,256]{2,1,0:T(2,128)S(1)}, u32[]{:S(2)}, u32[]{:S(2)}) %collective-permute-start.2) | collective-permute-done | bytes 32800 | tf_op jit(solution)/shard_map/ppermute | solution.py:438
  45.7 12.7 %grads.1 = (f32[9,256,128]{2,1,0:T(8,128)S(1)}, bf16[9,256,128]{2,1,0:T(8,128)(2,1)S(1)}, bf16[8,512,128]{2,1,0:T(8,128)(2,1)S(1)}) custom-call(s32[1]{0:T(128)} %bitcast.core_ref, s32[32]{0:T(128)S(1)} %select_reduce_fusion.2.order_ref, s32[1]{0:T(128)} %bitcast.12.units_ref, s32[140]{0:T(256)S(1)} %get-tuple-element.27.tile_ref, ...), custom_call_target="tpu_custom_call" | custom-call | flops 5368709120 | bytes 10485760 | tf_op jit(solution)/shard_map/grads/pallas_call | solution.py:330
  58.5 2.0 %collective-permute-done.3 = bf16[9,256,128]{2,1,0:T(8,128)(2,1)S(1)} collective-permute-done((bf16[9,256,128]{2,1,0:T(8,128)(2,1)S(1)}, bf16[9,256,128]{2,1,0:T(8,128)(2,1)S(1)}, u32[]{:S(2)}, u32[]{:S(2)}) %collective-permute-start.3) | collective-permute-done | bytes 589856 | tf_op jit(solution)/shard_map/ppermute | solution.py:445
  60.5 0.1 fusion.5
  60.6 0.1 pad_maximum_fusion
  60.7 24.3 %all_to_all.15.x_ref = bf16[8,768,128]{2,1,0:T(8,128)(2,1)S(1)} all-to-all(bf16[8,768,128]{2,1,0:T(8,128)(2,1)S(1)} %pad_maximum_fusion), channel_id=1, replica_groups={{0,8,16,24,32,40,48,56},{4,12,20,28,36,44,52,60},{1,9,17,25,33,41,49,57..., dimensions={0} | all-to-all | bytes 3145728 | tf_op jit(solution)/shard_map/all_to_all | solution.py:413
  85.0 1.2 %unpack.1 = (bf16[256,768]{1,0:T(8,128)(2,1)}, bf16[256,768]{1,0:T(8,128)(2,1)}, bf16[256,768]{1,0:T(8,128)(2,1)}) custom-call(bf16[8,768,128]{2,1,0:T(8,128)(2,1)S(1)} %all_to_all.15.x_ref), custom_call_target="tpu_custom_call" | custom-call | tf_op jit(solution)/shard_map/unpack/pallas_call | solution.py:65
  (34 shorter events, 1.1 us)
Async XLA Ops:
  0.6 7.6 %copy-start.3 = (s32[8]{0:T(128)S(1)}, s32[8]{0:T(128)}, u32[]{:S(2)}) copy-start(s32[8]{0:T(128)} %param.12) | copy-start | bytes 100
  2.9 5.7 %copy-start = (bf16[256,768]{1,0:T(8,128)(2,1)S(1)}, bf16[256,768]{1,0:T(8,128)(2,1)}, u32[]{:S(2)}) copy-start(bf16[256,768]{1,0:T(8,128)(2,1)} %param.11) | copy-start | bytes 1179652
  2.9 6.2 %copy-start.1 = (bf16[256,768]{1,0:T(8,128)(2,1)S(1)}, bf16[256,768]{1,0:T(8,128)(2,1)}, u32[]{:S(2)}) copy-start(bf16[256,768]{1,0:T(8,128)(2,1)} %param.9) | copy-start | bytes 1179652
  2.9 21.3 %all-to-all-start = ((bf16[8,528,128]{2,1,0:T(8,128)(2,1)}), bf16[8,528,128]{2,1,0:T(8,128)(2,1)S(1)}, u32[]{:S(2)}, u32[]{:S(2)}) async-start(bf16[8,528,128]{2,1,0:T(8,128)(2,1)} %pack.1), calls=%async_computation | async-start | bytes 2162688 | tf_op jit(solution)/shard_map/all_to_all | solution.py:413
  8.7 1.0 %copy-start.2 = (bf16[256,768]{1,0:T(8,128)(2,1)S(1)}, bf16[256,768]{1,0:T(8,128)(2,1)}, u32[]{:S(2)}) copy-start(bf16[256,768]{1,0:T(8,128)(2,1)} %param.10) | copy-start | bytes 1179652
  24.2 19.3 %all-to-all-start.1 = ((bf16[8,544,128]{2,1,0:T(8,128)(2,1)}), bf16[8,544,128]{2,1,0:T(8,128)(2,1)S(1)}, u32[]{:S(2)}, u32[]{:S(2)}) async-start(bf16[8,544,128]{2,1,0:T(8,128)(2,1)} %fusion.4), calls=%async_computation.1 | async-start | bytes 2228224 | tf_op jit(solution)/shard_map/all_to_all | solution.py:413
  27.8 2.0 %collective-permute-start = (bf16[8,272,128]{2,1,0:T(8,128)(2,1)S(1)}, bf16[8,272,128]{2,1,0:T(8,128)(2,1)S(1)}, u32[]{:S(2)}, u32[]{:S(2)}) collective-permute-start(bf16[8,272,128]{2,1,0:T(8,128)(2,1)S(1)} %slice.17), channel_id=1, source_target_pairs={{0,4},{4,0},{8,12},{12,8},{16,20},{20,16},{24,28},{28,24},{32,36},... | collective-permute-start | bytes 1671176 | tf_op jit(solution)/shard_map/ppermute | solution.py:429
  43.6 2.1 %collective-permute-start.1 = (bf16[8,288,128]{2,1,0:T(8,128)(2,1)S(1)}, bf16[8,288,128]{2,1,0:T(8,128)(2,1)S(1)}, u32[]{:S(2)}, u32[]{:S(2)}) collective-permute-start(bf16[8,288,128]{2,1,0:T(8,128)(2,1)S(1)} %slice.19), channel_id=1, source_target_pairs={{0,4},{4,0},{8,12},{12,8},{16,20},{20,16},{24,28},{28,24},{32,36},... | collective-permute-start | bytes 1769480 | tf_op jit(solution)/shard_map/ppermute | solution.py:440
  43.7 2.0 %collective-permute-start.2 = (f32[16,2,256]{2,1,0:T(2,128)S(1)}, f32[16,2,256]{2,1,0:T(2,128)S(1)}, u32[]{:S(2)}, u32[]{:S(2)}) collective-permute-start(f32[16,2,256]{2,1,0:T(2,128)S(1)} %get-tuple-element.16.stats_ref), channel_id=1, source_target_pairs={{0,4},{4,0},{8,12},{12,8},{16,20},{20,16},{24,28},{28,24},{32,36},... | collective-permute-start | bytes 98312 | tf_op jit(solution)/shard_map/ppermute | solution.py:438
  58.4 2.1 %collective-permute-start.3 = (bf16[9,256,128]{2,1,0:T(8,128)(2,1)S(1)}, bf16[9,256,128]{2,1,0:T(8,128)(2,1)S(1)}, u32[]{:S(2)}, u32[]{:S(2)}) collective-permute-start(bf16[9,256,128]{2,1,0:T(8,128)(2,1)S(1)} %get-tuple-element.19), channel_id=1, source_target_pairs={{0,4},{4,0},{8,12},{12,8},{16,20},{20,16},{24,28},{28,24},{32,36},... | collective-permute-start | bytes 1769480 | tf_op jit(solution)/shard_map/ppermute | solution.py:445
